TPU v7x, 1024 devices: a whole 4x8x16 slice. The times are simulated.
1024 devices in a mesh: ab: 128 (over y, z), cd: 8 (over x, core).
Axes of the slice: x: 4, y: 8, z: 16, core: 2. Of those that a mesh axis runs over, the one named last changes fastest.
Arguments:
- amplitudes: bfloat16 [2, 1024, 14336], P(None, 'ab', 'cd'), may hold values from -6 to 6
- integrals: bfloat16 [8, 14336, 14336], P(None, 'ab', 'cd'), may hold values from -0.046875 to 0.046875
- batch_irrep: int32 [2], replicated, may hold values from 0 to 7
- pair_fill: int32 [8], replicated, may hold values from 7168 to 14336
Outputs:
- residual: float32 [2, 1024, 14336], P(None, 'cd', 'ab')
All inputs are finite; a program needn't handle non-finite values.
Results may differ from a plain program's by a relative error of at most 0.00035.
Values may be sent and summed in bfloat16 or wider, within the bound.
No kernel may reach another device: no remote copies, remote signals or barrier semaphores. Data moves between devices by JAX's collectives and lax.ppermute only.
A program may use at most 32 MiB of HBM per device.

v0:
```python
import jax
import jax.numpy as jnp
from jax import lax
from jax.sharding import PartitionSpec as P


def on_device(amplitudes, integrals, batch_irrep, pair_fill):
    batches, own_pairs, cd_cols = amplitudes.shape
    ab_rows = integrals.shape[1]
    ab_place = lax.axis_index("ab")
    cd_place = lax.axis_index("cd")
    zero_half = jnp.zeros((), amplitudes.dtype)
    limits = pair_fill[batch_irrep]
    col_global = cd_place * cd_cols + jnp.arange(cd_cols, dtype=jnp.int32)
    row_global = ab_place * ab_rows + jnp.arange(ab_rows, dtype=jnp.int32)
    col_used = col_global[None, :] < limits[:, None]
    row_used = row_global[None, :] < limits[:, None]
    blocks = jnp.stack(
        [
            lax.dynamic_index_in_dim(integrals, batch_irrep[batch], 0, keepdims=False)
            for batch in range(batches)
        ]
    )
    weights = jnp.where(col_used[:, None, :], blocks, zero_half)
    partial_all = jnp.einsum(
        "bnc,brc->bnr",
        lax.all_gather(amplitudes, "ab", axis=1, tiled=True),
        weights,
        preferred_element_type=jnp.float32,
    )
    summed = lax.psum_scatter(partial_all, "cd", scatter_dimension=1, tiled=True)
    return jnp.where(row_used[:, None, :], summed, jnp.zeros((), jnp.float32))


def solution(mesh):
    placed = (P(None, "ab", "cd"), P(None, "ab", "cd"), P(), P())
    return jax.shard_map(
        on_device, mesh=mesh, in_specs=placed, out_specs=P(None, "cd", "ab"), check_vma=False
    )
```

profile of v0, /device:TPU:1, one launch (start us, length us, event | category | flops | bytes accessed | tf_op | source)
XLA Modules:
  0.0 226.9 jit_solution(3725865672851734517)
XLA Ops:
  6.5 0.0 copy-start
  6.5 0.0 all-gather.2.cloned.1.call-start
  6.5 0.7 all-gather.2.cloned.1.call-update
  7.3 0.0 reduce-scatter.2.cloned.1.call-start
  7.3 1.4 fusion.6
  12.5 0.7 compare_select_fusion
  13.2 0.0 copy-done
  13.2 0.6 gather_fusion
  13.8 1.2 constant_dynamic-slice_fusion.1
  15.0 0.1 broadcast_compare_fusion
  15.1 153.3 %all-gather.2.cloned.1.call-done = bf16[2,1024,1792]{2,1,0:T(8,128)(2,1)} async-done(((bf16[2,8,1792]{2,1,0:T(8,128)(2,1)}), bf16[2,1024,1792]{2,1,0:T(8,128)(2,1)}) %all-gather.2.cloned.1.call-update) | async-done | bytes 7340048 | tf_op jit(solution)/shard_map/all_gather | solution.py:27
  168.3 6.4 %convolution_bitcast_fusion = f32[2,1024,112]{1,2,0:T(8,128)} fusion(bf16[2,1024,1792]{2,1,0:T(8,128)(2,1)} %all-gather.2.cloned.1.call-done, bf16[1,112,1792]{2,1,0:T(8,128)(2,1)S(1)} %get-tuple-element.6, bf16[1,112,1792]{2,1,0:T(8,128)(2,1)S(1)} %get-tuple-element.5, pred[2,1792]{1,0:T(4,128)(4,1)S(1)} %broadcast_compare_fusion), kind=kOutput, calls=%fused_computation.1 | convolution fusion | flops 822886400 | bytes 9063936 | tf_op jit(solution)/shard_map/bnc,brc->bnr/dot_general | solution.py:25
  174.7 0.0 reduce-scatter.2.cloned.1.call-update
  174.8 0.1 broadcast_compare_fusion.1
  174.8 43.6 %reduce-scatter.2.cloned.1.call-done = f32[2,128,112]{1,2,0:T(8,128)} async-done(((f32[2,1024,112]{1,2,0:T(8,128)}), f32[2,128,112]{1,2,0:T(8,128)}) %reduce-scatter.2.cloned.1.call-update) | async-done | bytes 114704 | tf_op jit(solution)/shard_map/reduce_scatter | solution.py:31
  218.5 1.6 broadcast_select_fusion
  (3 shorter events, 0.0 us)
Async XLA Ops:
  6.5 6.6 %copy-start = (s32[8]{0:T(128)S(1)}, s32[8]{0:T(128)}, u32[]{:S(2)}) copy-start(s32[8]{0:T(128)} %param.7) | copy-start | bytes 100
  6.5 161.8 %all-gather.2.cloned.1.call-start = ((), (), s32[]{:S(2)}) async-start(), calls=%async_computation.1 | async-start | bytes 7397376 | tf_op jit(solution)/shard_map/all_gather | solution.py:27
  7.3 211.2 %reduce-scatter.2.cloned.1.call-start = ((), (), s32[]{:S(2)}) async-start(), calls=%async_computation.2 | async-start | bytes 1032192 | tf_op jit(solution)/shard_map/reduce_scatter | solution.py:31
Sparse Core Ops, SparseCore 0:
  11.5 156.7 all-gather.1
  174.9 43.5 reduce-scatter.1
where the time goes:
time: 227 us
  waiting for transfers between devices  198 us (87%)
  between operations  17.2 us (8%)
  matrix products  6.41 us (3%)
  local copies, waits for them, and re-layouts  3.18 us (1%)
  other arithmetic  2.47 us (1%)
    all_gather x1, waiting for transfers between devices, on_device(): lax.all_gather(amplitudes, 'ab', axis=1, tiled=True)  153 us
    reduce_scatter x1, waiting for transfers between devices, on_device(): lax.psum_scatter(partial_all, 'cd', scatter_dimension=1, tiled=True)  43.6 us
    dot_general x1, matrix products, on_device(): jnp.einsum('bnc,brc->bnr', lax.all_gather(amplitudes, 'ab', axis=1, tiled...  6.41 us
  transfers between devices with their start and end apart: 2, of which 2 were waited for; matrix products, arithmetic and copies ran while one was open for 2% of the time, Pallas kernels for 0%

commit v1 on v0

v1 whole, which is shorter than its diff:
```python
import jax
import jax.numpy as jnp
from jax import lax
from jax.experimental import pallas as pl
from jax.experimental.pallas import tpu as pltpu
from jax.sharding import Mesh, PartitionSpec as P

Y, ZA, ZB, X, C = 8, 4, 4, 4, 2
Z = ZA * ZB
ZAX = ("za", "zb")
LANES = 128
OFFSETS = (0, -1, 1, -2, 2, -3, 3, 4)


def shift(values, axis, size, step):
    return lax.ppermute(values, axis, [(i, (i + step) % size) for i in range(size)])


def swap_cores(values):
    return lax.ppermute(values, "c", [(0, 1), (1, 0)])


def pick_kernel(irrep_ref, integrals_ref, mine_ref, other_ref, sems):
    core = lax.axis_index("c")
    mine = pltpu.make_async_copy(integrals_ref.at[irrep_ref[core]], mine_ref, sems.at[0])
    other = pltpu.make_async_copy(integrals_ref.at[irrep_ref[1 - core]], other_ref, sems.at[1])
    mine.start()
    other.start()
    mine.wait()
    other.wait()


def pick(batch_irrep, integrals):
    block = jax.ShapeDtypeStruct(integrals.shape[1:], integrals.dtype)
    return pl.pallas_call(
        pick_kernel,
        out_shape=(block, block),
        in_specs=[pl.BlockSpec(memory_space=pltpu.SMEM), pl.BlockSpec(memory_space=pl.ANY)],
        out_specs=[pl.BlockSpec(memory_space=pltpu.VMEM)] * 2,
        scratch_shapes=[pltpu.SemaphoreType.DMA((2,))],
        cost_estimate=pl.CostEstimate(flops=0, bytes_accessed=2**21, transcendentals=0),
        name="pick_blocks",
    )(batch_irrep, integrals)


def ladder_kernel(irrep_ref, fill_ref, *refs):
    pairs, blocks = refs[: len(OFFSETS)], refs[len(OFFSETS) : len(OFFSETS) + 4]
    out_ref, left, right, left_sems, right_sems = refs[len(OFFSETS) + 4 :]
    halves, rows, cols = pairs[0].shape
    ab_rows = blocks[0].shape[1]
    y, x, core = lax.axis_index("y"), lax.axis_index("x"), lax.axis_index("c")

    left_loads = [
        pltpu.make_async_copy(
            pair.at[half], left.at[at, :, pl.ds(half * cols, cols)], left_sems.at[at, half]
        )
        for at, pair in enumerate(pairs)
        for half in range(halves)
    ]
    places = [pl.multiple_of(lax.rem(core + half, halves) * cols, LANES) for half in range(halves)]
    right_loads = [
        [
            pltpu.make_async_copy(
                block.at[half], right.at[at, pl.ds(0, ab_rows), pl.ds(places[half], cols)], right_sems.at[at, half]
            )
            for half in range(halves)
        ]
        for at, block in enumerate(blocks)
    ]
    for load in left_loads + right_loads[0] + right_loads[1] + right_loads[2] + right_loads[3]:
        load.start()
    for load in left_loads:
        load.wait()
    limit = fill_ref[irrep_ref[core]]
    place = x * halves * cols + lax.broadcasted_iota(jnp.int32, (1, halves * cols), 1)
    every = left[...].reshape(len(pairs) * rows, halves * cols)
    every = jnp.where(place < limit, every, jnp.zeros((), every.dtype))
    for pair in range(2):
        for load in right_loads[2 * pair] + right_loads[2 * pair + 1]:
            load.wait()
        weight = right[pl.ds(2 * pair, 2)].reshape(2 * LANES, halves * cols)
        product = lax.dot_general(
            every, weight, (((1,), (1,)), ((), ())), preferred_element_type=jnp.float32
        )
        for at, offset in enumerate(OFFSETS):
            owner = lax.rem(y + offset + Y, Y)
            for part in range(2):
                out_ref[owner, 2 * pair + part] = product[
                    at * rows : (at + 1) * rows, part * LANES : part * LANES + ab_rows
                ]


def partial_ladder(batch_irrep, pair_fill, pairs, blocks):
    halves, rows, cols = pairs[0].shape
    owners, ab_rows = len(pairs), blocks[0].shape[1]
    flops = 2 * owners * rows * 4 * ab_rows * halves * cols
    return pl.pallas_call(
        ladder_kernel,
        out_shape=jax.ShapeDtypeStruct((owners, 4, rows, ab_rows), jnp.float32),
        in_specs=[pl.BlockSpec(memory_space=pltpu.SMEM)] * 2
        + [pl.BlockSpec(memory_space=pl.ANY)] * (owners + 4),
        out_specs=pl.BlockSpec(memory_space=pltpu.VMEM),
        scratch_shapes=[
            pltpu.VMEM((owners, rows, halves * cols), jnp.bfloat16),
            pltpu.VMEM((4, LANES, halves * cols), jnp.bfloat16),
            pltpu.SemaphoreType.DMA((owners, halves)),
            pltpu.SemaphoreType.DMA((4, halves)),
        ],
        compiler_params=pltpu.CompilerParams(vmem_limit_bytes=56 * 2**20),
        cost_estimate=pl.CostEstimate(flops=flops, bytes_accessed=6 * 2**20, transcendentals=0),
        name="partial_ladder",
    )(batch_irrep, pair_fill, *pairs, *blocks)


def on_device(amplitudes, integrals, batch_irrep, pair_fill):
    batches, own_pairs, cd_cols = amplitudes.shape
    ab_rows = integrals.shape[1]
    y_place = lax.axis_index("y")
    z_place = lax.axis_index(ZAX)
    limits = pair_fill[batch_irrep]

    def of_batch(values, n):
        return lax.dynamic_index_in_dim(values, n, 0, keepdims=False)

    mine, other = pick(batch_irrep, integrals)
    other = swap_cores(other)
    spread = jnp.broadcast_to(amplitudes[None], (ZA, *amplitudes.shape)).reshape(ZA * C, own_pairs, cd_cols)
    own = lax.all_to_all(spread, ("za", "c"), 0, 0, tiled=True)
    own = own.reshape(ZA, C, own_pairs, cd_cols).transpose(1, 0, 2, 3).reshape(C, ZA * own_pairs, cd_cols)
    mid = jnp.stack([mine, other])
    own, mid = lax.optimization_barrier((own, mid))

    low1 = shift(mid, ZAX, Z, 1)
    right1, left1 = shift(own, "y", Y, 1), shift(own, "y", Y, -1)
    right2, left2 = shift(right1, "y", Y, 1), shift(left1, "y", Y, -1)
    mid, left2 = lax.optimization_barrier((mid, left2))
    high1 = shift(mid, ZAX, Z, -1)
    right3, left3 = shift(right2, "y", Y, 1), shift(left2, "y", Y, -1)
    low1, right3 = lax.optimization_barrier((low1, right3))
    low2 = shift(low1, ZAX, Z, 1)
    right4 = shift(right3, "y", Y, 1)
    pairs = [own, right1, left1, right2, left2, right3, left3, right4]

    partial = partial_ladder(batch_irrep, pair_fill, pairs, [low2, low1, mid, high1])
    parts = lax.all_to_all(partial, ("x", "c"), 0, 0, tiled=True)
    total = jnp.sum(parts.reshape(X, C, *parts.shape[1:]), axis=0)

    pieces = jnp.stack(
        [
            total[:, 2],
            shift(total[:, 1], ZAX, Z, -1),
            shift(total[:, 0], ZAX, Z, -2),
            shift(total[:, 3], ZAX, Z, 1),
        ]
    )
    z_class = lax.rem(z_place, ZB)
    classes = [of_batch(pieces, lax.rem(b - z_class + ZB, ZB)) for b in range(ZB)]
    ladder = jnp.stack([piece.reshape(batches, ZA, own_pairs, ab_rows) for piece in classes], axis=2)
    ladder = ladder.reshape(batches, ZA * ZB * own_pairs, ab_rows)
    row_used = (y_place * Z + z_place) * ab_rows + jnp.arange(ab_rows, dtype=jnp.int32) < limits[:, None]
    return jnp.where(row_used[:, None, :], ladder, jnp.zeros((), jnp.float32))


def solution(mesh):
    whole = Mesh(mesh.devices.reshape(Y, ZA, ZB, X, C), ("y", "za", "zb", "x", "c"))
    placed = (P(None, ("y", "za", "zb"), ("x", "c")),) * 2 + (P(), P())
    return jax.shard_map(
        on_device,
        mesh=whole,
        in_specs=placed,
        out_specs=P(None, ("x", "c"), ("y", "za", "zb")),
        check_vma=False,
    )
```

time: 227 us -> 129 us (0.57)
  waiting for transfers between devices: 198 us -> 45.5 us
  starting transfers between devices: 0.04 us -> 68.6 us
  between operations: 17.2 us -> 0.31 us
  Pallas kernels: 0 us -> 9.17 us
  matrix products: 6.41 us -> 0 us
    all_gather x1 -> x0, waiting for transfers between devices: 153 us -> none  [on_device(): lax.all_gather(amplitudes, 'ab', axis=1, tiled=True)]
    reduce_scatter x1 -> x0, waiting for transfers between devices: 43.6 us -> none  [on_device(): lax.psum_scatter(partial_all, 'cd', scatter_dimension=1, tiled=True)]
    ppermute x0 -> x14, starting transfers between devices: none -> 39.9 us  [the longest x13 38 us: shift(): lax.ppermute(values, axis, [(i, (i + step) % size) for i in range(size)])]
    all_to_all x0 -> x2, starting transfers between devices: none -> 28.7 us  [the longest x1 20.2 us: on_device(): own = lax.all_to_all(spread, ('za', 'c'), 0, 0, tiled=True)]
    ppermute x0 -> x14, waiting for transfers between devices: none -> 23.1 us  [the longest x13 21.2 us: shift(): lax.ppermute(values, axis, [(i, (i + step) % size) for i in range(size)])]
    all_to_all x0 -> x2, waiting for transfers between devices: none -> 22.4 us  [the longest x1 13.6 us: on_device(): own = lax.all_to_all(spread, ('za', 'c'), 0, 0, tiled=True)]
    pallas_call x0 -> x2, Pallas kernels: none -> 9.17 us  [the longest x1 6.46 us: partial_ladder(): pl.pallas_call(ladder_kernel, out_shape=jax.ShapeDtypeStruct((owners, 4,...]
    dot_general x1 -> x0, matrix products: 6.41 us -> none  [on_device(): jnp.einsum('bnc,brc->bnr', lax.all_gather(amplitudes, 'ab', axis=1, tiled...]
  transfers between devices with their start and end apart: 2 -> 16, of which waited for: 2 -> 10; matrix products, arithmetic and copies ran while one was open for 2% -> 1% of each run, Pallas kernels for 0% -> 2%
where the time goes in v1:
time: 129 us; the launch traced here: 128 us
  starting transfers between devices  68.6 us (53%)
  waiting for transfers between devices  45.5 us (35%)
  Pallas kernels  9.17 us (7%)
  local copies, waits for them, and re-layouts  3.01 us (2%)
    ppermute x13, starting transfers between devices, shift(): lax.ppermute(values, axis, [(i, (i + step) % size) for i in range(size)])  38 us
    ppermute x13, waiting for transfers between devices, shift(): lax.ppermute(values, axis, [(i, (i + step) % size) for i in range(size)])  21.2 us
    all_to_all x1, starting transfers between devices, on_device(): own = lax.all_to_all(spread, ('za', 'c'), 0, 0, tiled=True)  20.2 us
    all_to_all x1, waiting for transfers between devices, on_device(): own = lax.all_to_all(spread, ('za', 'c'), 0, 0, tiled=True)  13.6 us
    all_to_all x1, waiting for transfers between devices, on_device(): parts = lax.all_to_all(partial, ('x', 'c'), 0, 0, tiled=True)  8.81 us
    all_to_all x1, starting transfers between devices, on_device(): parts = lax.all_to_all(partial, ('x', 'c'), 0, 0, tiled=True)  8.43 us
    pallas_call x1, Pallas kernels, partial_ladder(): pl.pallas_call(ladder_kernel, out_shape=jax.ShapeDtypeStruct((owners, 4,...  6.46 us
    pallas_call x1, Pallas kernels, pick(): pl.pallas_call(pick_kernel, out_shape=(block, block), in_specs=[pl.BlockS...  2.71 us
  transfers between devices with their start and end apart: 16, of which 10 were waited for; matrix products, arithmetic and copies ran while one was open for 1% of the time, Pallas kernels for 2%

profile of v1, /device:TPU:1, one launch (start us, length us, event | category | flops | bytes accessed | tf_op | source)
XLA Modules:
  0.0 127.8 jit_solution(13752742060637729370)
XLA Ops:
  1.5 20.2 %all-to-all-start = ((bf16[8,8,1792]{2,1,0:T(8,128)(2,1)}), bf16[8,8,1792]{2,1,0:T(8,128)(2,1)S(1)}, u32[]{:S(2)}, u32[]{:S(2)}) async-start(bf16[8,8,1792]{2,1,0:T(8,128)(2,1)} %bitcast), calls=%async_computation | async-start | bytes 458752 | tf_op jit(solution)/shard_map/all_to_all | solution.py:128
  21.8 2.7 %pick_blocks.1 = (bf16[112,1792]{1,0:T(8,128)(2,1)}, bf16[112,1792]{1,0:T(8,128)(2,1)}) custom-call(s32[2]{0:T(128)} %irrep_ref.3, bf16[8,112,1792]{2,1,0:T(8,128)(2,1)} %integrals_ref.1), custom_call_target="tpu_custom_call" | custom-call | bytes 2097152 | tf_op jit(solution)/shard_map/pick_blocks/pallas_call | solution.py:35
  29.4 13.6 %all-to-all-done = bf16[8,8,1792]{2,1,0:T(8,128)(2,1)S(1)} async-done(((bf16[8,8,1792]{2,1,0:T(8,128)(2,1)}), bf16[8,8,1792]{2,1,0:T(8,128)(2,1)S(1)}, u32[]{:S(2)}, u32[]{:S(2)}) %all-to-all-start) | async-done | bytes 229408 | tf_op jit(solution)/shard_map/all_to_all | solution.py:128
  43.0 1.9 %collective-permute-start.5 = (bf16[2,112,1792]{2,1,0:T(8,128)(2,1)S(1)}, bf16[2,112,1792]{2,1,0:T(8,128)(2,1)S(1)}, u32[]{:S(2)}, u32[]{:S(2)}) collective-permute-start(bf16[2,112,1792]{2,1,0:T(8,128)(2,1)S(1)} %pad_maximum_fusion.refs_10_), channel_id=1, source_target_pairs={{0,8},{8,16},{16,24},{24,32},{32,40},{40,48},{48,56},{56,64},{64,7... | collective-permute-start | bytes 2408456 | tf_op jit(solution)/shard_map/ppermute | solution.py:16
  44.9 3.2 %collective-permute-start.1 = (bf16[2,32,1792]{2,1,0:T(8,128)(2,1)S(1)}, bf16[2,32,1792]{2,1,0:T(8,128)(2,1)S(1)}, u32[]{:S(2)}, u32[]{:S(2)}) collective-permute-start(bf16[2,32,1792]{2,1,0:T(8,128)(2,1)S(1)} %bitcast.39), channel_id=1, source_target_pairs={{0,128},{128,256},{256,384},{384,512},{512,640},{640,768},{768,896... | collective-permute-start | bytes 688136 | tf_op jit(solution)/shard_map/ppermute | solution.py:16
  48.2 3.8 %collective-permute-start.2 = (bf16[2,32,1792]{2,1,0:T(8,128)(2,1)S(1)}, bf16[2,32,1792]{2,1,0:T(8,128)(2,1)S(1)}, u32[]{:S(2)}, u32[]{:S(2)}) collective-permute-start(bf16[2,32,1792]{2,1,0:T(8,128)(2,1)S(1)} %bitcast.40), channel_id=1, source_target_pairs={{0,896},{128,0},{256,128},{384,256},{512,384},{640,512},{768,640},... | collective-permute-start | bytes 688136 | tf_op jit(solution)/shard_map/ppermute | solution.py:16
  52.0 3.5 %collective-permute-done.1.refs_1_ = bf16[2,32,1792]{2,1,0:T(8,128)(2,1)S(1)} collective-permute-done((bf16[2,32,1792]{2,1,0:T(8,128)(2,1)S(1)}, bf16[2,32,1792]{2,1,0:T(8,128)(2,1)S(1)}, u32[]{:S(2)}, u32[]{:S(2)}) %collective-permute-start.1) | collective-permute-done | bytes 229408 | tf_op jit(solution)/shard_map/ppermute | solution.py:16
  57.4 4.6 %collective-permute-start.4 = (bf16[2,32,1792]{2,1,0:T(8,128)(2,1)S(1)}, bf16[2,32,1792]{2,1,0:T(8,128)(2,1)}, u32[]{:S(2)}, u32[]{:S(2)}) collective-permute-start(bf16[2,32,1792]{2,1,0:T(8,128)(2,1)S(1)} %collective-permute-done.2.refs_2_), channel_id=1, source_target_pairs={{0,896},{128,0},{256,128},{384,256},{512,384},{640,512},{768,640},... | collective-permute-start | bytes 688136 | tf_op jit(solution)/shard_map/ppermute | solution.py:16
  62.0 2.5 %collective-permute-done.3.refs_3_ = bf16[2,32,1792]{2,1,0:T(8,128)(2,1)S(1)} collective-permute-done((bf16[2,32,1792]{2,1,0:T(8,128)(2,1)S(1)}, bf16[2,32,1792]{2,1,0:T(8,128)(2,1)S(1)}, u32[]{:S(2)}, u32[]{:S(2)}) %collective-permute-start.3) | collective-permute-done | bytes 229408 | tf_op jit(solution)/shard_map/ppermute | solution.py:16
  66.5 3.9 %collective-permute-start.10 = (bf16[2,112,1792]{2,1,0:T(8,128)(2,1)S(1)}, bf16[2,112,1792]{2,1,0:T(8,128)(2,1)S(1)}, u32[]{:S(2)}, u32[]{:S(2)}) collective-permute-start(bf16[2,112,1792]{2,1,0:T(8,128)(2,1)S(1)} %pad_maximum_fusion.refs_10_), channel_id=1, source_target_pairs={{0,120},{8,0},{16,8},{24,16},{32,24},{40,32},{48,40},{56,48},{64,5... | collective-permute-start | bytes 2408456 | tf_op jit(solution)/shard_map/ppermute | solution.py:16
  70.4 2.2 %collective-permute-done.6.refs_5_ = bf16[2,32,1792]{2,1,0:T(8,128)(2,1)} collective-permute-done((bf16[2,32,1792]{2,1,0:T(8,128)(2,1)S(1)}, bf16[2,32,1792]{2,1,0:T(8,128)(2,1)}, u32[]{:S(2)}, u32[]{:S(2)}) %collective-permute-start.6) | collective-permute-done | bytes 229408 | tf_op jit(solution)/shard_map/ppermute | solution.py:16
  72.6 3.0 %collective-permute-start.9 = (bf16[2,112,1792]{2,1,0:T(8,128)(2,1)S(1)}, bf16[2,112,1792]{2,1,0:T(8,128)(2,1)}, u32[]{:S(2)}, u32[]{:S(2)}) collective-permute-start(bf16[2,112,1792]{2,1,0:T(8,128)(2,1)S(1)} %collective-permute-done.5.refs_9_), channel_id=1, source_target_pairs={{0,8},{8,16},{16,24},{24,32},{32,40},{40,48},{48,56},{56,64},{64,7... | collective-permute-start | bytes 2408456 | tf_op jit(solution)/shard_map/ppermute | solution.py:16
  75.6 1.9 %collective-permute-start.7 = (bf16[2,32,1792]{2,1,0:T(8,128)(2,1)}, bf16[2,32,1792]{2,1,0:T(8,128)(2,1)}, u32[]{:S(2)}, u32[]{:S(2)}) collective-permute-start(bf16[2,32,1792]{2,1,0:T(8,128)(2,1)} %collective-permute-done.4.refs_4_), channel_id=1, source_target_pairs={{0,896},{128,0},{256,128},{384,256},{512,384},{640,512},{768,640},... | collective-permute-start | bytes 688136 | tf_op jit(solution)/shard_map/ppermute | solution.py:16
  77.6 3.4 %collective-permute-start.8 = (bf16[2,32,1792]{2,1,0:T(8,128)(2,1)}, bf16[2,32,1792]{2,1,0:T(8,128)(2,1)}, u32[]{:S(2)}, u32[]{:S(2)}) collective-permute-start(bf16[2,32,1792]{2,1,0:T(8,128)(2,1)} %collective-permute-done.6.refs_5_), channel_id=1, source_target_pairs={{0,128},{128,256},{256,384},{384,512},{512,640},{640,768},{768,896... | collective-permute-start | bytes 688136 | tf_op jit(solution)/shard_map/ppermute | solution.py:16
  81.0 2.0 %collective-permute-done.7.refs_6_ = bf16[2,32,1792]{2,1,0:T(8,128)(2,1)} collective-permute-done((bf16[2,32,1792]{2,1,0:T(8,128)(2,1)}, bf16[2,32,1792]{2,1,0:T(8,128)(2,1)}, u32[]{:S(2)}, u32[]{:S(2)}) %collective-permute-start.7) | collective-permute-done | bytes 229408 | tf_op jit(solution)/shard_map/ppermute | solution.py:16
  83.0 3.1 %collective-permute-done.8.refs_7_ = bf16[2,32,1792]{2,1,0:T(8,128)(2,1)} collective-permute-done((bf16[2,32,1792]{2,1,0:T(8,128)(2,1)}, bf16[2,32,1792]{2,1,0:T(8,128)(2,1)}, u32[]{:S(2)}, u32[]{:S(2)}) %collective-permute-start.8) | collective-permute-done | bytes 229408 | tf_op jit(solution)/shard_map/ppermute | solution.py:16
  86.2 5.8 %collective-permute-done.9.refs_8_ = bf16[2,112,1792]{2,1,0:T(8,128)(2,1)} collective-permute-done((bf16[2,112,1792]{2,1,0:T(8,128)(2,1)S(1)}, bf16[2,112,1792]{2,1,0:T(8,128)(2,1)}, u32[]{:S(2)}, u32[]{:S(2)}) %collective-permute-start.9) | collective-permute-done | bytes 802848 | tf_op jit(solution)/shard_map/ppermute | solution.py:16
  92.0 6.5 %partial_ladder.1 = f32[8,4,32,112]{3,2,1,0:T(8,128)} custom-call(s32[2]{0:T(128)} %irrep_ref.3, s32[8]{0:T(128)} %fill_ref.1, bf16[2,32,1792]{2,1,0:T(8,128)(2,1)} %bitcast.41, bf16[2,32,1792]{2,1,0:T(8,128)(2,1)} %copy-done.5, bf16[2,32,1792]{2,1,0:T(8,128)(2,1)} %copy-done.6, bf16[2,32,1792]{2,1,0:T(8,128)(2,1)} %copy-done.7, ...), custom_call_target="tpu_custom_call" | custom-call | flops 822083584 | bytes 6291456 | tf_op jit(solution)/shard_map/partial_ladder/pallas_call | solution.py:97
  98.5 8.4 %all-to-all-start.1 = ((f32[8,4,32,112]{3,2,1,0:T(8,128)}), f32[8,4,32,112]{3,2,1,0:T(8,128)S(1)}, u32[]{:S(2)}, u32[]{:S(2)}) async-start(f32[8,4,32,112]{3,2,1,0:T(8,128)} %partial_ladder.1), calls=%async_computation.1 | async-start | bytes 1048576 | tf_op jit(solution)/shard_map/all_to_all | solution.py:145
  107.6 8.8 %all-to-all-done.1 = f32[8,4,32,112]{3,2,1,0:T(8,128)S(1)} async-done(((f32[8,4,32,112]{3,2,1,0:T(8,128)}), f32[8,4,32,112]{3,2,1,0:T(8,128)S(1)}, u32[]{:S(2)}, u32[]{:S(2)}) %all-to-all-start.1) | async-done | bytes 458784 | tf_op jit(solution)/shard_map/all_to_all | solution.py:145
  116.5 1.9 %collective-permute-start.12 = (f32[2,32,112]{2,1,0:T(8,128)S(1)}, f32[2,32,112]{2,1,0:T(8,128)S(1)}, u32[]{:S(2)}, u32[]{:S(2)}) collective-permute-start(f32[2,32,112]{2,1,0:T(8,128)S(1)} %get-tuple-element.28), channel_id=1, source_target_pairs={{0,112},{8,120},{16,0},{24,8},{32,16},{40,24},{48,32},{56,40},{64,... | collective-permute-start | bytes 86024 | tf_op jit(solution)/shard_map/ppermute | solution.py:16
  118.4 3.9 %collective-permute-start.13 = (f32[2,32,112]{2,1,0:T(8,128)S(1)}, f32[2,32,112]{2,1,0:T(8,128)S(1)}, u32[]{:S(2)}, u32[]{:S(2)}) collective-permute-start(f32[2,32,112]{2,1,0:T(8,128)S(1)} %get-tuple-element.27), channel_id=1, source_target_pairs={{0,8},{8,16},{16,24},{24,32},{32,40},{40,48},{48,56},{56,64},{64,7... | collective-permute-start | bytes 86024 | tf_op jit(solution)/shard_map/ppermute | solution.py:16
  122.3 2.6 %collective-permute-start.11 = (f32[2,32,112]{2,1,0:T(8,128)S(1)}, f32[2,32,112]{2,1,0:T(8,128)S(1)}, u32[]{:S(2)}, u32[]{:S(2)}) collective-permute-start(f32[2,32,112]{2,1,0:T(8,128)S(1)} %get-tuple-element.26), channel_id=1, source_target_pairs={{0,120},{8,0},{16,8},{24,16},{32,24},{40,32},{48,40},{56,48},{64,5... | collective-permute-start | bytes 86024 | tf_op jit(solution)/shard_map/ppermute | solution.py:16
  125.0 2.0 %collective-permute-done.11 = f32[2,32,112]{2,1,0:T(8,128)S(1)} collective-permute-done((f32[2,32,112]{2,1,0:T(8,128)S(1)}, f32[2,32,112]{2,1,0:T(8,128)S(1)}, u32[]{:S(2)}, u32[]{:S(2)}) %collective-permute-start.11) | collective-permute-done | bytes 28704 | tf_op jit(solution)/shard_map/ppermute | solution.py:16
  (44 shorter events, 11.9 us)
Async XLA Ops:
  1.5 41.5 %all-to-all-start = ((bf16[8,8,1792]{2,1,0:T(8,128)(2,1)}), bf16[8,8,1792]{2,1,0:T(8,128)(2,1)S(1)}, u32[]{:S(2)}, u32[]{:S(2)}) async-start(bf16[8,8,1792]{2,1,0:T(8,128)(2,1)} %bitcast), calls=%async_computation | async-start | bytes 458752 | tf_op jit(solution)/shard_map/all_to_all | solution.py:128
  24.5 3.8 %collective-permute-start = (bf16[112,1792]{1,0:T(8,128)(2,1)}, bf16[112,1792]{1,0:T(8,128)(2,1)S(1)}, u32[]{:S(2)}, u32[]{:S(2)}) collective-permute-start(bf16[112,1792]{1,0:T(8,128)(2,1)} %get-tuple-element.14), channel_id=1, source_target_pairs={{0,1},{1,0},{2,3},{3,2},{4,5},{5,4},{6,7},{7,6},{8,9},{9,8},{10,11... | collective-permute-start | bytes 1204232 | tf_op jit(solution)/shard_map/ppermute | solution.py:20
  29.4 62.6 %copy-start.1 = (bf16[2,112,1792]{2,1,0:T(8,128)(2,1)}, bf16[2,112,1792]{2,1,0:T(8,128)(2,1)S(1)}, u32[]{:S(2)}) copy-start(bf16[2,112,1792]{2,1,0:T(8,128)(2,1)S(1)} %pad_maximum_fusion.refs_10_) | copy-start | bytes 2408452
  43.0 49.0 %copy-start.2 = (bf16[2,4,8,1792]{3,2,1,0:T(8,128)(2,1)}, bf16[2,4,8,1792]{3,2,1,0:T(8,128)(2,1)S(1)}, u32[]{:S(2)}) copy-start(bf16[2,4,8,1792]{3,2,1,0:T(8,128)(2,1)S(1)} %copy.18) | copy-start | bytes 688132
  43.0 29.6 %collective-permute-start.5 = (bf16[2,112,1792]{2,1,0:T(8,128)(2,1)S(1)}, bf16[2,112,1792]{2,1,0:T(8,128)(2,1)S(1)}, u32[]{:S(2)}, u32[]{:S(2)}) collective-permute-start(bf16[2,112,1792]{2,1,0:T(8,128)(2,1)S(1)} %pad_maximum_fusion.refs_10_), channel_id=1, source_target_pairs={{0,8},{8,16},{16,24},{24,32},{32,40},{40,48},{48,56},{56,64},{64,7... | collective-permute-start | bytes 2408456 | tf_op jit(solution)/shard_map/ppermute | solution.py:16
  44.9 10.5 %collective-permute-start.1 = (bf16[2,32,1792]{2,1,0:T(8,128)(2,1)S(1)}, bf16[2,32,1792]{2,1,0:T(8,128)(2,1)S(1)}, u32[]{:S(2)}, u32[]{:S(2)}) collective-permute-start(bf16[2,32,1792]{2,1,0:T(8,128)(2,1)S(1)} %bitcast.39), channel_id=1, source_target_pairs={{0,128},{128,256},{256,384},{384,512},{512,640},{640,768},{768,896... | collective-permute-start | bytes 688136 | tf_op jit(solution)/shard_map/ppermute | solution.py:16
  48.2 9.2 %collective-permute-start.2 = (bf16[2,32,1792]{2,1,0:T(8,128)(2,1)S(1)}, bf16[2,32,1792]{2,1,0:T(8,128)(2,1)S(1)}, u32[]{:S(2)}, u32[]{:S(2)}) collective-permute-start(bf16[2,32,1792]{2,1,0:T(8,128)(2,1)S(1)} %bitcast.40), channel_id=1, source_target_pairs={{0,896},{128,0},{256,128},{384,256},{512,384},{640,512},{768,640},... | collective-permute-start | bytes 688136 | tf_op jit(solution)/shard_map/ppermute | solution.py:16
  55.5 36.5 %copy-start.5 = (bf16[2,32,1792]{2,1,0:T(8,128)(2,1)}, bf16[2,32,1792]{2,1,0:T(8,128)(2,1)S(1)}, u32[]{:S(2)}) copy-start(bf16[2,32,1792]{2,1,0:T(8,128)(2,1)S(1)} %collective-permute-done.1.refs_1_) | copy-start | bytes 688132
  55.5 9.1 %collective-permute-start.3 = (bf16[2,32,1792]{2,1,0:T(8,128)(2,1)S(1)}, bf16[2,32,1792]{2,1,0:T(8,128)(2,1)S(1)}, u32[]{:S(2)}, u32[]{:S(2)}) collective-permute-start(bf16[2,32,1792]{2,1,0:T(8,128)(2,1)S(1)} %collective-permute-done.1.refs_1_), channel_id=1, source_target_pairs={{0,128},{128,256},{256,384},{384,512},{512,640},{640,768},{768,896... | collective-permute-start | bytes 688136 | tf_op jit(solution)/shard_map/ppermute | solution.py:16
  57.4 34.6 %copy-start.6 = (bf16[2,32,1792]{2,1,0:T(8,128)(2,1)}, bf16[2,32,1792]{2,1,0:T(8,128)(2,1)S(1)}, u32[]{:S(2)}) copy-start(bf16[2,32,1792]{2,1,0:T(8,128)(2,1)S(1)} %collective-permute-done.2.refs_2_) | copy-start | bytes 688132
  57.4 9.0 %collective-permute-start.4 = (bf16[2,32,1792]{2,1,0:T(8,128)(2,1)S(1)}, bf16[2,32,1792]{2,1,0:T(8,128)(2,1)}, u32[]{:S(2)}, u32[]{:S(2)}) collective-permute-start(bf16[2,32,1792]{2,1,0:T(8,128)(2,1)S(1)} %collective-permute-done.2.refs_2_), channel_id=1, source_target_pairs={{0,896},{128,0},{256,128},{384,256},{512,384},{640,512},{768,640},... | collective-permute-start | bytes 688136 | tf_op jit(solution)/shard_map/ppermute | solution.py:16
  64.5 27.5 %copy-start.7 = (bf16[2,32,1792]{2,1,0:T(8,128)(2,1)}, bf16[2,32,1792]{2,1,0:T(8,128)(2,1)S(1)}, u32[]{:S(2)}) copy-start(bf16[2,32,1792]{2,1,0:T(8,128)(2,1)S(1)} %collective-permute-done.3.refs_3_) | copy-start | bytes 688132
  64.5 8.1 %collective-permute-start.6 = (bf16[2,32,1792]{2,1,0:T(8,128)(2,1)S(1)}, bf16[2,32,1792]{2,1,0:T(8,128)(2,1)}, u32[]{:S(2)}, u32[]{:S(2)}) collective-permute-start(bf16[2,32,1792]{2,1,0:T(8,128)(2,1)S(1)} %collective-permute-done.3.refs_3_), channel_id=1, source_target_pairs={{0,128},{128,256},{256,384},{384,512},{512,640},{640,768},{768,896... | collective-permute-start | bytes 688136 | tf_op jit(solution)/shard_map/ppermute | solution.py:16
  66.5 19.7 %collective-permute-start.10 = (bf16[2,112,1792]{2,1,0:T(8,128)(2,1)S(1)}, bf16[2,112,1792]{2,1,0:T(8,128)(2,1)S(1)}, u32[]{:S(2)}, u32[]{:S(2)}) collective-permute-start(bf16[2,112,1792]{2,1,0:T(8,128)(2,1)S(1)} %pad_maximum_fusion.refs_10_), channel_id=1, source_target_pairs={{0,120},{8,0},{16,8},{24,16},{32,24},{40,32},{48,40},{56,48},{64,5... | collective-permute-start | bytes 2408456 | tf_op jit(solution)/shard_map/ppermute | solution.py:16
  72.6 19.4 %copy-start.3 = (bf16[2,112,1792]{2,1,0:T(8,128)(2,1)}, bf16[2,112,1792]{2,1,0:T(8,128)(2,1)S(1)}, u32[]{:S(2)}) copy-start(bf16[2,112,1792]{2,1,0:T(8,128)(2,1)S(1)} %collective-permute-done.5.refs_9_) | copy-start | bytes 2408452
  72.6 19.4 %collective-permute-start.9 = (bf16[2,112,1792]{2,1,0:T(8,128)(2,1)S(1)}, bf16[2,112,1792]{2,1,0:T(8,128)(2,1)}, u32[]{:S(2)}, u32[]{:S(2)}) collective-permute-start(bf16[2,112,1792]{2,1,0:T(8,128)(2,1)S(1)} %collective-permute-done.5.refs_9_), channel_id=1, source_target_pairs={{0,8},{8,16},{16,24},{24,32},{32,40},{40,48},{48,56},{56,64},{64,7... | collective-permute-start | bytes 2408456 | tf_op jit(solution)/shard_map/ppermute | solution.py:16
  75.6 7.4 %collective-permute-start.7 = (bf16[2,32,1792]{2,1,0:T(8,128)(2,1)}, bf16[2,32,1792]{2,1,0:T(8,128)(2,1)}, u32[]{:S(2)}, u32[]{:S(2)}) collective-permute-start(bf16[2,32,1792]{2,1,0:T(8,128)(2,1)} %collective-permute-done.4.refs_4_), channel_id=1, source_target_pairs={{0,896},{128,0},{256,128},{384,256},{512,384},{640,512},{768,640},... | collective-permute-start | bytes 688136 | tf_op jit(solution)/shard_map/ppermute | solution.py:16
  77.6 8.6 %collective-permute-start.8 = (bf16[2,32,1792]{2,1,0:T(8,128)(2,1)}, bf16[2,32,1792]{2,1,0:T(8,128)(2,1)}, u32[]{:S(2)}, u32[]{:S(2)}) collective-permute-start(bf16[2,32,1792]{2,1,0:T(8,128)(2,1)} %collective-permute-done.6.refs_5_), channel_id=1, source_target_pairs={{0,128},{128,256},{256,384},{384,512},{512,640},{640,768},{768,896... | collective-permute-start | bytes 688136 | tf_op jit(solution)/shard_map/ppermute | solution.py:16
  81.0 26.0 %copy-start.8 = (s32[2]{0:T(128)S(1)}, s32[2]{0:T(128)}, u32[]{:S(2)}) copy-start(s32[2]{0:T(128)} %irrep_ref.3) | copy-start | bytes 28
  81.0 26.0 %copy-start = (s32[8]{0:T(128)S(1)}, s32[8]{0:T(128)}, u32[]{:S(2)}) copy-start(s32[8]{0:T(128)} %fill_ref.1) | copy-start | bytes 100
  98.5 17.9 %all-to-all-start.1 = ((f32[8,4,32,112]{3,2,1,0:T(8,128)}), f32[8,4,32,112]{3,2,1,0:T(8,128)S(1)}, u32[]{:S(2)}, u32[]{:S(2)}) async-start(f32[8,4,32,112]{3,2,1,0:T(8,128)} %partial_ladder.1), calls=%async_computation.1 | async-start | bytes 1048576 | tf_op jit(solution)/shard_map/all_to_all | solution.py:145
  116.5 8.5 %collective-permute-start.12 = (f32[2,32,112]{2,1,0:T(8,128)S(1)}, f32[2,32,112]{2,1,0:T(8,128)S(1)}, u32[]{:S(2)}, u32[]{:S(2)}) collective-permute-start(f32[2,32,112]{2,1,0:T(8,128)S(1)} %get-tuple-element.28), channel_id=1, source_target_pairs={{0,112},{8,120},{16,0},{24,8},{32,16},{40,24},{48,32},{56,40},{64,... | collective-permute-start | bytes 86024 | tf_op jit(solution)/shard_map/ppermute | solution.py:16
  118.4 6.6 %collective-permute-start.13 = (f32[2,32,112]{2,1,0:T(8,128)S(1)}, f32[2,32,112]{2,1,0:T(8,128)S(1)}, u32[]{:S(2)}, u32[]{:S(2)}) collective-permute-start(f32[2,32,112]{2,1,0:T(8,128)S(1)} %get-tuple-element.27), channel_id=1, source_target_pairs={{0,8},{8,16},{16,24},{24,32},{32,40},{40,48},{48,56},{56,64},{64,7... | collective-permute-start | bytes 86024 | tf_op jit(solution)/shard_map/ppermute | solution.py:16
  122.3 4.7 %collective-permute-start.11 = (f32[2,32,112]{2,1,0:T(8,128)S(1)}, f32[2,32,112]{2,1,0:T(8,128)S(1)}, u32[]{:S(2)}, u32[]{:S(2)}) collective-permute-start(f32[2,32,112]{2,1,0:T(8,128)S(1)} %get-tuple-element.26), channel_id=1, source_target_pairs={{0,120},{8,0},{16,8},{24,16},{32,24},{40,32},{48,40},{56,48},{64,5... | collective-permute-start | bytes 86024 | tf_op jit(solution)/shard_map/ppermute | solution.py:16
  (1 other events, 5.9 us)

commit v2 on v0

v2 whole, which is shorter than its diff:
```python
import jax
import jax.numpy as jnp
from jax import lax
from jax.experimental import pallas as pl
from jax.experimental.pallas import tpu as pltpu
from jax.sharding import Mesh, PartitionSpec as P

Y, ZA, H, PAR, X, C = 8, 4, 2, 2, 4, 2
AXES = ("y", "za", "h", "par", "x", "c")
QUAD = H * PAR
LANES = 128
TOP = 14


def trade(values, first):
    pairs = []
    for even in range(0, Y, 2):
        other = (even + 1 - 2 * first) % Y
        pairs += [(even, other), (other, even)]
    return lax.ppermute(values, "y", pairs)


def owner_of(y, part, at):
    step = (0, 1, -1, -2, 2, 3, -3, -4)[at]
    side = 1 - 2 * lax.rem(y + part, 2)
    return lax.rem(y + side * step + Y, Y)


def pick_kernel(irrep_ref, integrals_ref, out_ref, sems):
    cols = out_ref.shape[-1]
    copies = [
        pltpu.make_async_copy(
            integrals_ref.at[irrep_ref[n], :, pl.ds(h * cols, cols)], out_ref.at[h, par, n], sems.at[h, par, n]
        )
        for h in range(H)
        for par in range(PAR)
        for n in range(C)
    ]
    for copy in copies:
        copy.start()
    for copy in copies:
        copy.wait()


def pick(batch_irrep, integrals):
    ab_rows, cols = integrals.shape[1:]
    return pl.pallas_call(
        pick_kernel,
        out_shape=jax.ShapeDtypeStruct((H, PAR, C, ab_rows, cols // H), integrals.dtype),
        in_specs=[pl.BlockSpec(memory_space=pltpu.SMEM), pl.BlockSpec(memory_space=pl.ANY)],
        out_specs=pl.BlockSpec(memory_space=pltpu.VMEM),
        scratch_shapes=[pltpu.SemaphoreType.DMA((H, PAR, C))],
        cost_estimate=pl.CostEstimate(flops=0, bytes_accessed=2**21, transcendentals=0),
        name="pick_blocks",
    )(batch_irrep, integrals)


def ladder_kernel(irrep_ref, fill_ref, *refs):
    pairs, blocks_ref = refs[: 4 * C], refs[4 * C]
    out_ref, left, right = refs[4 * C + 1 :]
    _, rows, cols = pairs[0].shape
    parts, ab_rows = blocks_ref.shape[1:3]
    y, x, h, core = (lax.axis_index(axis) for axis in ("y", "x", "h", "c"))

    limit = fill_ref[irrep_ref[core]]
    for part in range(parts):
        place = ((x * C + part) * H + h) * cols + lax.broadcasted_iota(jnp.int32, (1, cols), 1)
        used = place < limit
        for at in range(Y):
            values = pairs[part * 4 + at // 2][at % 2]
            left[part, owner_of(y, part, at)] = jnp.where(used, values, jnp.zeros((), values.dtype))
    for at in range(QUAD):
        for part in range(parts):
            right[part, at, pl.ds(0, ab_rows)] = blocks_ref[at, part]
    column = lax.broadcasted_iota(jnp.int32, (1, LANES), 1)
    for half in range(QUAD // 2):
        product = sum(
            lax.dot_general(
                left[part].reshape(Y * rows, cols),
                right[part, pl.ds(2 * half, 2)].reshape(2 * LANES, cols),
                (((1,), (1,)), ((), ())),
                preferred_element_type=jnp.float32,
            )
            for part in range(parts)
        )
        for side in range(2):
            tile = product[:, side * LANES : (side + 1) * LANES]
            tile = jnp.where(column < ab_rows, tile, jnp.zeros((), jnp.float32))
            peak = jnp.max(jnp.abs(tile), axis=1, keepdims=True)
            power = jnp.clip(jnp.ceil(jnp.log2(jnp.maximum(peak, 1e-37))), -112.0, 112.0)
            scaled = jnp.where(column == ab_rows, power, tile * jnp.exp2(TOP - power))
            whole = jnp.floor(scaled + 0.5).astype(jnp.int32).astype(jnp.int16)
            out_ref[2 * half + side] = whole.reshape(Y, rows, LANES)


def total_kernel(irrep_ref, fill_ref, parts_ref, out_ref):
    batches, ab_rows, _ = out_ref.shape
    rows = parts_ref.shape[1]
    place = lax.axis_index("y")
    for axis, size in (("za", ZA), ("h", H), ("par", PAR)):
        place = place * size + lax.axis_index(axis)
    ab = place * ab_rows + lax.broadcasted_iota(jnp.int32, (ab_rows, 1), 0)
    for n in range(batches):
        classes = []
        for par in range(PAR):
            total = jnp.zeros((rows, LANES), jnp.float32)
            for h in range(H):
                for x in range(X):
                    part = parts_ref[((h * PAR + par) * X + x) * C + n].astype(jnp.float32)
                    total += part * jnp.exp2(part[:, ab_rows : ab_rows + 1] - TOP)
            classes.append(total)
        eight = rows // (ZA * H)
        pieces = [
            classes[par][at * eight : (at + 1) * eight] for at in range(ZA * H) for par in range(PAR)
        ]
        turned = jnp.concatenate(pieces, axis=0).T[:ab_rows]
        out_ref[n] = jnp.where(ab < fill_ref[irrep_ref[n]], turned, jnp.zeros((), jnp.float32))


def total_ladder(batch_irrep, pair_fill, parts, batches, ab_rows):
    return pl.pallas_call(
        total_kernel,
        out_shape=jax.ShapeDtypeStruct((batches, ab_rows, PAR * parts.shape[1]), jnp.float32),
        in_specs=[pl.BlockSpec(memory_space=pltpu.SMEM)] * 2 + [pl.BlockSpec(memory_space=pltpu.VMEM)],
        out_specs=pl.BlockSpec(memory_space=pltpu.VMEM),
        cost_estimate=pl.CostEstimate(flops=2**20, bytes_accessed=2**20, transcendentals=0),
        name="total_ladder",
    )(batch_irrep, pair_fill, parts)


def partial_ladder(batch_irrep, pair_fill, pairs, blocks):
    _, rows, cols = pairs[0].shape
    parts, ab_rows = blocks.shape[1:3]
    owners = Y
    flops = 2 * owners * rows * QUAD * ab_rows * parts * cols
    return pl.pallas_call(
        ladder_kernel,
        out_shape=jax.ShapeDtypeStruct((QUAD, owners, rows, LANES), jnp.int16),
        in_specs=[pl.BlockSpec(memory_space=pltpu.SMEM)] * 2
        + [pl.BlockSpec(memory_space=pltpu.VMEM)] * (len(pairs) + 1),
        out_specs=pl.BlockSpec(memory_space=pltpu.VMEM),
        scratch_shapes=[
            pltpu.VMEM((parts, owners, rows, cols), jnp.bfloat16),
            pltpu.VMEM((parts, QUAD, LANES, cols), jnp.bfloat16),
        ],
        compiler_params=pltpu.CompilerParams(vmem_limit_bytes=24 * 2**20),
        cost_estimate=pl.CostEstimate(flops=flops, bytes_accessed=6 * 2**20, transcendentals=0),
        name="partial_ladder",
    )(batch_irrep, pair_fill, *pairs, blocks)


def on_device(amplitudes, integrals, batch_irrep, pair_fill):
    batches, own_pairs, cd_cols = amplitudes.shape
    ab_rows = integrals.shape[1]
    cols = cd_cols // H

    spread = amplitudes.reshape(batches, own_pairs, H, cols).transpose(2, 0, 1, 3)
    spread = jnp.broadcast_to(spread[None], (ZA, H, C, own_pairs, cols)).reshape(-1, own_pairs, cols)
    own = lax.all_to_all(spread, ("za", "h", "c"), 0, 0, tiled=True)
    own = own.reshape(ZA, H, C, own_pairs, cols).transpose(2, 0, 1, 3, 4).reshape(C, ZA * H * own_pairs, cols)

    picked = pick(batch_irrep, integrals).reshape(-1, ab_rows, cols)
    blocks = lax.all_to_all(picked, ("h", "par", "c"), 0, 0, tiled=True).reshape(QUAD, C, ab_rows, cols)

    pairs = [[], []]
    held = [own[0][None], own[1][None]]
    for step in range(4):
        for part in range(C):
            came = trade(held[part], (step + part) % 2)
            if step == 0:
                came = jnp.concatenate([held[part], came], axis=0)
            held[part] = came
            pairs[part].append(came)
    pairs = pairs[0] + pairs[1]

    partial = partial_ladder(batch_irrep, pair_fill, pairs, blocks)
    partial = partial.reshape(-1, *partial.shape[2:])
    parts = lax.all_to_all(partial, ("h", "par", "x", "c"), 0, 0, tiled=True)
    return total_ladder(batch_irrep, pair_fill, parts, batches, ab_rows).swapaxes(1, 2)


def solution(mesh):
    whole = Mesh(mesh.devices.reshape(Y, ZA, H, PAR, X, C), AXES)
    placed = (P(None, AXES[:4], AXES[4:]),) * 2 + (P(), P())
    return jax.shard_map(
        on_device, mesh=whole, in_specs=placed, out_specs=P(None, AXES[4:], AXES[:4]), check_vma=False
    )
```

time: 227 us -> 114 us (0.50)
  waiting for transfers between devices: 198 us -> 30.3 us
  starting transfers between devices: 0.04 us -> 47.7 us
  blocking collectives: 0 us -> 25.2 us
  between operations: 17.2 us -> 0.11 us
  Pallas kernels: 0 us -> 8.01 us
  matrix products: 6.41 us -> 0 us
  other arithmetic: 2.47 us -> 0.05 us
    all_gather x1 -> x0, waiting for transfers between devices: 153 us -> none  [on_device(): lax.all_gather(amplitudes, 'ab', axis=1, tiled=True)]
    reduce_scatter x1 -> x0, waiting for transfers between devices: 43.6 us -> none  [on_device(): lax.psum_scatter(partial_all, 'cd', scatter_dimension=1, tiled=True)]
    all_to_all x0 -> x1, blocking collectives: none -> 25.2 us  [on_device(): parts = lax.all_to_all(partial, ('h', 'par', 'x', 'c'), 0, 0, tiled=True)]
    all_to_all x0 -> x2, starting transfers between devices: none -> 23.9 us  [the longest x1 20.3 us: on_device(): own = lax.all_to_all(spread, ('za', 'h', 'c'), 0, 0, tiled=True)]
    ppermute x0 -> x8, starting transfers between devices: none -> 23.8 us  [trade(): return lax.ppermute(values, 'y', pairs)]
    all_to_all x0 -> x2, waiting for transfers between devices: none -> 16.1 us  [the longest x1 16.1 us: on_device(): own = lax.all_to_all(spread, ('za', 'h', 'c'), 0, 0, tiled=True)]
    ppermute x0 -> x8, waiting for transfers between devices: none -> 14.2 us  [trade(): return lax.ppermute(values, 'y', pairs)]
    pallas_call x0 -> x3, Pallas kernels: none -> 8.01 us  [the longest x1 3.39 us: pick(): pl.pallas_call(pick_kernel, out_shape=jax.ShapeDtypeStruct((H, PAR, C, ab...]
  transfers between devices with their start and end apart: 2 -> 10, of which waited for: 2 -> 9; matrix products, arithmetic and copies ran while one was open for 2% -> 0% of each run, Pallas kernels for 0% -> 3%
where the time goes in v2:
time: 114 us; the launch traced here: 113 us
  starting transfers between devices  47.7 us (42%)
  waiting for transfers between devices  30.3 us (27%)
  blocking collectives  25.2 us (22%)
  Pallas kernels  8.01 us (7%)
  local copies, waits for them, and re-layouts  1.57 us (1%)
    all_to_all x1, blocking collectives, on_device(): parts = lax.all_to_all(partial, ('h', 'par', 'x', 'c'), 0, 0, tiled=True)  25.2 us
    ppermute x8, starting transfers between devices, trade(): return lax.ppermute(values, 'y', pairs)  23.8 us
    all_to_all x1, starting transfers between devices, on_device(): own = lax.all_to_all(spread, ('za', 'h', 'c'), 0, 0, tiled=True)  20.3 us
    all_to_all x1, waiting for transfers between devices, on_device(): own = lax.all_to_all(spread, ('za', 'h', 'c'), 0, 0, tiled=True)  16.1 us
    ppermute x8, waiting for transfers between devices, trade(): return lax.ppermute(values, 'y', pairs)  14.2 us
    all_to_all x1, starting transfers between devices, on_device(): lax.all_to_all(picked, ('h', 'par', 'c'), 0, 0, tiled=True)  3.66 us
    pallas_call x1, Pallas kernels, pick(): pl.pallas_call(pick_kernel, out_shape=jax.ShapeDtypeStruct((H, PAR, C, ab...  3.39 us
    pallas_call x1, Pallas kernels, partial_ladder(): pl.pallas_call(ladder_kernel, out_shape=jax.ShapeDtypeStruct((QUAD, owner...  2.48 us
  transfers between devices with their start and end apart: 10, of which 9 were waited for; matrix products, arithmetic and copies ran while one was open for 0% of the time, Pallas kernels for 3%

profile of v2, /device:TPU:1, one launch (start us, length us, event | category | flops | bytes accessed | tf_op | source)
XLA Modules:
  0.0 113.0 jit_solution(11782093295026485320)
XLA Ops:
  0.0 0.8 copy.6
  0.8 0.7 broadcast_in_dim.2
  1.5 20.3 %all-to-all-start = ((bf16[16,8,896]{2,1,0:T(8,128)(2,1)}), bf16[16,8,896]{2,1,0:T(8,128)(2,1)S(1)}, u32[]{:S(2)}, u32[]{:S(2)}) async-start(bf16[16,8,896]{2,1,0:T(8,128)(2,1)} %bitcast.2), calls=%async_computation | async-start | bytes 458752 | tf_op jit(solution)/shard_map/all_to_all | solution.py:159
  21.8 3.4 %pick_blocks.1 = bf16[2,2,2,112,896]{4,3,2,1,0:T(8,128)(2,1)} custom-call(s32[2]{0:T(128)} %irrep_ref.5, bf16[8,112,1792]{2,1,0:T(8,128)(2,1)} %integrals_ref.1), custom_call_target="tpu_custom_call" | custom-call | bytes 2097152 | tf_op jit(solution)/shard_map/pick_blocks/pallas_call | solution.py:47
  25.2 16.1 %all-to-all-done = bf16[16,8,896]{2,1,0:T(8,128)(2,1)S(1)} async-done(((bf16[16,8,896]{2,1,0:T(8,128)(2,1)}), bf16[16,8,896]{2,1,0:T(8,128)(2,1)S(1)}, u32[]{:S(2)}, u32[]{:S(2)}) %all-to-all-start) | async-done | bytes 229408 | tf_op jit(solution)/shard_map/all_to_all | solution.py:159
  41.3 3.7 %all-to-all-start.1 = ((bf16[8,112,896]{2,1,0:T(8,128)(2,1)}), bf16[8,112,896]{2,1,0:T(8,128)(2,1)S(1)}, u32[]{:S(2)}, u32[]{:S(2)}) async-start(bf16[8,112,896]{2,1,0:T(8,128)(2,1)} %bitcast.15), calls=%async_computation.1 | async-start | bytes 3211264 | tf_op jit(solution)/shard_map/all_to_all | solution.py:163
  45.0 5.1 %collective-permute-start.4 = (bf16[1,64,896]{2,1,0:T(8,128)(2,1)S(1)}, bf16[1,64,896]{2,1,0:T(8,128)(2,1)S(1)}, u32[]{:S(2)}, u32[]{:S(2)}) collective-permute-start(bf16[1,64,896]{2,1,0:T(8,128)(2,1)S(1)} %bitcast.19), channel_id=1, source_target_pairs={{0,896},{896,0},{256,128},{128,256},{512,384},{384,512},{768,640},... | collective-permute-start | bytes 344072 | tf_op jit(solution)/shard_map/ppermute | solution.py:20
  50.1 1.9 %collective-permute-start = (bf16[1,64,896]{2,1,0:T(8,128)(2,1)S(1)}, bf16[1,64,896]{2,1,0:T(8,128)(2,1)S(1)}, u32[]{:S(2)}, u32[]{:S(2)}) collective-permute-start(bf16[1,64,896]{2,1,0:T(8,128)(2,1)S(1)} %bitcast.17), channel_id=1, source_target_pairs={{0,128},{128,0},{256,384},{384,256},{512,640},{640,512},{768,896},... | collective-permute-start | bytes 344072 | tf_op jit(solution)/shard_map/ppermute | solution.py:20
  52.1 0.8 collective-permute-done.4
  52.9 2.5 %collective-permute-start.5 = (bf16[2,64,896]{2,1,0:T(8,128)(2,1)S(1)}, bf16[2,64,896]{2,1,0:T(8,128)(2,1)S(1)}, u32[]{:S(2)}, u32[]{:S(2)}) collective-permute-start(bf16[2,64,896]{2,1,0:T(8,128)(2,1)S(1)} %pad_maximum_fusion.1.refs_4_), channel_id=1, source_target_pairs={{0,128},{128,0},{256,384},{384,256},{512,640},{640,512},{768,896},... | collective-permute-start | bytes 688136 | tf_op jit(solution)/shard_map/ppermute | solution.py:20
  55.5 1.5 %collective-permute-done = bf16[1,64,896]{2,1,0:T(8,128)(2,1)S(1)} collective-permute-done((bf16[1,64,896]{2,1,0:T(8,128)(2,1)S(1)}, bf16[1,64,896]{2,1,0:T(8,128)(2,1)S(1)}, u32[]{:S(2)}, u32[]{:S(2)}) %collective-permute-start) | collective-permute-done | bytes 114720 | tf_op jit(solution)/shard_map/ppermute | solution.py:20
  57.0 2.7 %collective-permute-start.1 = (bf16[2,64,896]{2,1,0:T(8,128)(2,1)S(1)}, bf16[2,64,896]{2,1,0:T(8,128)(2,1)S(1)}, u32[]{:S(2)}, u32[]{:S(2)}) collective-permute-start(bf16[2,64,896]{2,1,0:T(8,128)(2,1)S(1)} %pad_maximum_fusion.refs_0_), channel_id=1, source_target_pairs={{0,896},{896,0},{256,128},{128,256},{512,384},{384,512},{768,640},... | collective-permute-start | bytes 688136 | tf_op jit(solution)/shard_map/ppermute | solution.py:20
  59.8 2.4 %collective-permute-done.5.refs_5_ = bf16[2,64,896]{2,1,0:T(8,128)(2,1)S(1)} collective-permute-done((bf16[2,64,896]{2,1,0:T(8,128)(2,1)S(1)}, bf16[2,64,896]{2,1,0:T(8,128)(2,1)S(1)}, u32[]{:S(2)}, u32[]{:S(2)}) %collective-permute-start.5) | collective-permute-done | bytes 229408 | tf_op jit(solution)/shard_map/ppermute | solution.py:20
  62.2 4.6 %collective-permute-start.6 = (bf16[2,64,896]{2,1,0:T(8,128)(2,1)S(1)}, bf16[2,64,896]{2,1,0:T(8,128)(2,1)S(1)}, u32[]{:S(2)}, u32[]{:S(2)}) collective-permute-start(bf16[2,64,896]{2,1,0:T(8,128)(2,1)S(1)} %collective-permute-done.5.refs_5_), channel_id=1, source_target_pairs={{0,896},{896,0},{256,128},{128,256},{512,384},{384,512},{768,640},... | collective-permute-start | bytes 688136 | tf_op jit(solution)/shard_map/ppermute | solution.py:20
  67.2 1.9 %collective-permute-start.2 = (bf16[2,64,896]{2,1,0:T(8,128)(2,1)S(1)}, bf16[2,64,896]{2,1,0:T(8,128)(2,1)S(1)}, u32[]{:S(2)}, u32[]{:S(2)}) collective-permute-start(bf16[2,64,896]{2,1,0:T(8,128)(2,1)S(1)} %collective-permute-done.1.refs_1_), channel_id=1, source_target_pairs={{0,128},{128,0},{256,384},{384,256},{512,640},{640,512},{768,896},... | collective-permute-start | bytes 688136 | tf_op jit(solution)/shard_map/ppermute | solution.py:20
  69.1 2.7 %collective-permute-done.6.refs_6_ = bf16[2,64,896]{2,1,0:T(8,128)(2,1)S(1)} collective-permute-done((bf16[2,64,896]{2,1,0:T(8,128)(2,1)S(1)}, bf16[2,64,896]{2,1,0:T(8,128)(2,1)S(1)}, u32[]{:S(2)}, u32[]{:S(2)}) %collective-permute-start.6) | collective-permute-done | bytes 229408 | tf_op jit(solution)/shard_map/ppermute | solution.py:20
  71.7 2.2 %collective-permute-start.7 = (bf16[2,64,896]{2,1,0:T(8,128)(2,1)S(1)}, bf16[2,64,896]{2,1,0:T(8,128)(2,1)S(1)}, u32[]{:S(2)}, u32[]{:S(2)}) collective-permute-start(bf16[2,64,896]{2,1,0:T(8,128)(2,1)S(1)} %collective-permute-done.6.refs_6_), channel_id=1, source_target_pairs={{0,128},{128,0},{256,384},{384,256},{512,640},{640,512},{768,896},... | collective-permute-start | bytes 688136 | tf_op jit(solution)/shard_map/ppermute | solution.py:20
  74.0 1.2 %collective-permute-done.2.refs_2_ = bf16[2,64,896]{2,1,0:T(8,128)(2,1)S(1)} collective-permute-done((bf16[2,64,896]{2,1,0:T(8,128)(2,1)S(1)}, bf16[2,64,896]{2,1,0:T(8,128)(2,1)S(1)}, u32[]{:S(2)}, u32[]{:S(2)}) %collective-permute-start.2) | collective-permute-done | bytes 229408 | tf_op jit(solution)/shard_map/ppermute | solution.py:20
  75.2 2.8 %collective-permute-start.3 = (bf16[2,64,896]{2,1,0:T(8,128)(2,1)S(1)}, bf16[2,64,896]{2,1,0:T(8,128)(2,1)S(1)}, u32[]{:S(2)}, u32[]{:S(2)}) collective-permute-start(bf16[2,64,896]{2,1,0:T(8,128)(2,1)S(1)} %collective-permute-done.2.refs_2_), channel_id=1, source_target_pairs={{0,896},{896,0},{256,128},{128,256},{512,384},{384,512},{768,640},... | collective-permute-start | bytes 688136 | tf_op jit(solution)/shard_map/ppermute | solution.py:20
  77.9 1.9 %collective-permute-done.7.refs_7_ = bf16[2,64,896]{2,1,0:T(8,128)(2,1)S(1)} collective-permute-done((bf16[2,64,896]{2,1,0:T(8,128)(2,1)S(1)}, bf16[2,64,896]{2,1,0:T(8,128)(2,1)S(1)}, u32[]{:S(2)}, u32[]{:S(2)}) %collective-permute-start.7) | collective-permute-done | bytes 229408 | tf_op jit(solution)/shard_map/ppermute | solution.py:20
  79.8 3.3 %collective-permute-done.3.refs_3_ = bf16[2,64,896]{2,1,0:T(8,128)(2,1)S(1)} collective-permute-done((bf16[2,64,896]{2,1,0:T(8,128)(2,1)S(1)}, bf16[2,64,896]{2,1,0:T(8,128)(2,1)S(1)}, u32[]{:S(2)}, u32[]{:S(2)}) %collective-permute-start.3) | collective-permute-done | bytes 229408 | tf_op jit(solution)/shard_map/ppermute | solution.py:20
  83.1 2.5 %partial_ladder.1 = s16[4,8,64,128]{3,2,1,0:T(8,128)(2,1)S(1)} custom-call(s32[2]{0:T(128)S(1)} %copy-done, s32[8]{0:T(128)S(1)} %copy-done.1, bf16[2,64,896]{2,1,0:T(8,128)(2,1)S(1)} %pad_maximum_fusion.refs_0_, bf16[2,64,896]{2,1,0:T(8,128)(2,1)S(1)} %collective-permute-done.1.refs_1_, bf16[2,64,896]{2,1,0:T(8,128)(2,1)S(1)} %collective-permute-done.2.refs_2_, ...), custom_call_target="tpu_custom_call" | custom-call | flops 822083584 | bytes 6291456 | tf_op jit(solution)/shard_map/partial_ladder/pallas_call | solution.py:136
  85.6 25.2 %all_to_all.15.parts_ref = s16[32,64,128]{2,1,0:T(8,128)(2,1)} all-to-all(s16[32,64,128]{2,1,0:T(8,128)(2,1)S(1)} %bitcast.14), channel_id=1, replica_groups=mesh['y'=8,'za'=4,'h'=2,'par'=2,'x'=4,'c'=2] {'h','par','x','c'}, dimensions={0} | all-to-all | bytes 1048576 | tf_op jit(solution)/shard_map/all_to_all | solution.py:178
  110.8 2.1 %total_ladder.1 = f32[2,112,128]{2,1,0:T(8,128)} custom-call(s32[2]{0:T(128)} %irrep_ref.5, s32[8]{0:T(128)} %fill_ref.3, s16[32,64,128]{2,1,0:T(8,128)(2,1)} %all_to_all.15.parts_ref), custom_call_target="tpu_custom_call" | custom-call | flops 1048576 | bytes 1048576 | tf_op jit(solution)/shard_map/total_ladder/pallas_call | solution.py:121
  (9 shorter events, 0.5 us)
Async XLA Ops:
  1.5 39.8 %all-to-all-start = ((bf16[16,8,896]{2,1,0:T(8,128)(2,1)}), bf16[16,8,896]{2,1,0:T(8,128)(2,1)S(1)}, u32[]{:S(2)}, u32[]{:S(2)}) async-start(bf16[16,8,896]{2,1,0:T(8,128)(2,1)} %bitcast.2), calls=%async_computation | async-start | bytes 458752 | tf_op jit(solution)/shard_map/all_to_all | solution.py:159
  41.3 41.8 %copy-start = (s32[2]{0:T(128)S(1)}, s32[2]{0:T(128)}, u32[]{:S(2)}) copy-start(s32[2]{0:T(128)} %irrep_ref.5) | copy-start | bytes 28
  41.3 41.8 %copy-start.1 = (s32[8]{0:T(128)S(1)}, s32[8]{0:T(128)}, u32[]{:S(2)}) copy-start(s32[8]{0:T(128)} %fill_ref.3) | copy-start | bytes 100
  41.3 41.8 %all-to-all-start.1 = ((bf16[8,112,896]{2,1,0:T(8,128)(2,1)}), bf16[8,112,896]{2,1,0:T(8,128)(2,1)S(1)}, u32[]{:S(2)}, u32[]{:S(2)}) async-start(bf16[8,112,896]{2,1,0:T(8,128)(2,1)} %bitcast.15), calls=%async_computation.1 | async-start | bytes 3211264 | tf_op jit(solution)/shard_map/all_to_all | solution.py:163
  45.0 7.9 %collective-permute-start.4 = (bf16[1,64,896]{2,1,0:T(8,128)(2,1)S(1)}, bf16[1,64,896]{2,1,0:T(8,128)(2,1)S(1)}, u32[]{:S(2)}, u32[]{:S(2)}) collective-permute-start(bf16[1,64,896]{2,1,0:T(8,128)(2,1)S(1)} %bitcast.19), channel_id=1, source_target_pairs={{0,896},{896,0},{256,128},{128,256},{512,384},{384,512},{768,640},... | collective-permute-start | bytes 344072 | tf_op jit(solution)/shard_map/ppermute | solution.py:20
  50.1 6.9 %collective-permute-start = (bf16[1,64,896]{2,1,0:T(8,128)(2,1)S(1)}, bf16[1,64,896]{2,1,0:T(8,128)(2,1)S(1)}, u32[]{:S(2)}, u32[]{:S(2)}) collective-permute-start(bf16[1,64,896]{2,1,0:T(8,128)(2,1)S(1)} %bitcast.17), channel_id=1, source_target_pairs={{0,128},{128,0},{256,384},{384,256},{512,640},{640,512},{768,896},... | collective-permute-start | bytes 344072 | tf_op jit(solution)/shard_map/ppermute | solution.py:20
  52.9 9.2 %collective-permute-start.5 = (bf16[2,64,896]{2,1,0:T(8,128)(2,1)S(1)}, bf16[2,64,896]{2,1,0:T(8,128)(2,1)S(1)}, u32[]{:S(2)}, u32[]{:S(2)}) collective-permute-start(bf16[2,64,896]{2,1,0:T(8,128)(2,1)S(1)} %pad_maximum_fusion.1.refs_4_), channel_id=1, source_target_pairs={{0,128},{128,0},{256,384},{384,256},{512,640},{640,512},{768,896},... | collective-permute-start | bytes 688136 | tf_op jit(solution)/shard_map/ppermute | solution.py:20
  57.0 10.1 %collective-permute-start.1 = (bf16[2,64,896]{2,1,0:T(8,128)(2,1)S(1)}, bf16[2,64,896]{2,1,0:T(8,128)(2,1)S(1)}, u32[]{:S(2)}, u32[]{:S(2)}) collective-permute-start(bf16[2,64,896]{2,1,0:T(8,128)(2,1)S(1)} %pad_maximum_fusion.refs_0_), channel_id=1, source_target_pairs={{0,896},{896,0},{256,128},{128,256},{512,384},{384,512},{768,640},... | collective-permute-start | bytes 688136 | tf_op jit(solution)/shard_map/ppermute | solution.py:20
  62.2 9.6 %collective-permute-start.6 = (bf16[2,64,896]{2,1,0:T(8,128)(2,1)S(1)}, bf16[2,64,896]{2,1,0:T(8,128)(2,1)S(1)}, u32[]{:S(2)}, u32[]{:S(2)}) collective-permute-start(bf16[2,64,896]{2,1,0:T(8,128)(2,1)S(1)} %collective-permute-done.5.refs_5_), channel_id=1, source_target_pairs={{0,896},{896,0},{256,128},{128,256},{512,384},{384,512},{768,640},... | collective-permute-start | bytes 688136 | tf_op jit(solution)/shard_map/ppermute | solution.py:20
  67.2 8.0 %collective-permute-start.2 = (bf16[2,64,896]{2,1,0:T(8,128)(2,1)S(1)}, bf16[2,64,896]{2,1,0:T(8,128)(2,1)S(1)}, u32[]{:S(2)}, u32[]{:S(2)}) collective-permute-start(bf16[2,64,896]{2,1,0:T(8,128)(2,1)S(1)} %collective-permute-done.1.refs_1_), channel_id=1, source_target_pairs={{0,128},{128,0},{256,384},{384,256},{512,640},{640,512},{768,896},... | collective-permute-start | bytes 688136 | tf_op jit(solution)/shard_map/ppermute | solution.py:20
  71.7 8.1 %collective-permute-start.7 = (bf16[2,64,896]{2,1,0:T(8,128)(2,1)S(1)}, bf16[2,64,896]{2,1,0:T(8,128)(2,1)S(1)}, u32[]{:S(2)}, u32[]{:S(2)}) collective-permute-start(bf16[2,64,896]{2,1,0:T(8,128)(2,1)S(1)} %collective-permute-done.6.refs_6_), channel_id=1, source_target_pairs={{0,128},{128,0},{256,384},{384,256},{512,640},{640,512},{768,896},... | collective-permute-start | bytes 688136 | tf_op jit(solution)/shard_map/ppermute | solution.py:20
  75.2 8.0 %collective-permute-start.3 = (bf16[2,64,896]{2,1,0:T(8,128)(2,1)S(1)}, bf16[2,64,896]{2,1,0:T(8,128)(2,1)S(1)}, u32[]{:S(2)}, u32[]{:S(2)}) collective-permute-start(bf16[2,64,896]{2,1,0:T(8,128)(2,1)S(1)} %collective-permute-done.2.refs_2_), channel_id=1, source_target_pairs={{0,896},{896,0},{256,128},{128,256},{512,384},{384,512},{768,640},... | collective-permute-start | bytes 688136 | tf_op jit(solution)/shard_map/ppermute | solution.py:20

commit v3 on v2

--- a/solution.py
+++ b/solution.py
@@ -9,7 +9,7 @@
 AXES = ("y", "za", "h", "par", "x", "c")
 QUAD = H * PAR
 LANES = 128
-TOP = 14
+TOP = 15
 
 
 def trade(values, first):
@@ -87,7 +87,7 @@
             tile = product[:, side * LANES : (side + 1) * LANES]
             tile = jnp.where(column < ab_rows, tile, jnp.zeros((), jnp.float32))
             peak = jnp.max(jnp.abs(tile), axis=1, keepdims=True)
-            power = jnp.clip(jnp.ceil(jnp.log2(jnp.maximum(peak, 1e-37))), -112.0, 112.0)
+            power = jnp.clip(jnp.ceil(jnp.log2(jnp.maximum(peak * 1.0001, 1e-37))), -111.0, 111.0)
             scaled = jnp.where(column == ab_rows, power, tile * jnp.exp2(TOP - power))
             whole = jnp.floor(scaled + 0.5).astype(jnp.int32).astype(jnp.int16)
             out_ref[2 * half + side] = whole.reshape(Y, rows, LANES)

time: 114 us -> 114 us (level)
  no operation moved by 1% of the time
where the time goes in v3:
time: 114 us; the launch traced here: 113 us
  starting transfers between devices  47.7 us (42%)
  waiting for transfers between devices  30.3 us (27%)
  blocking collectives  25.2 us (22%)
  Pallas kernels  8.01 us (7%)
  local copies, waits for them, and re-layouts  1.57 us (1%)
    all_to_all x1, blocking collectives, on_device(): parts = lax.all_to_all(partial, ('h', 'par', 'x', 'c'), 0, 0, tiled=True)  25.2 us
    ppermute x8, starting transfers between devices, trade(): return lax.ppermute(values, 'y', pairs)  23.8 us
    all_to_all x1, starting transfers between devices, on_device(): own = lax.all_to_all(spread, ('za', 'h', 'c'), 0, 0, tiled=True)  20.3 us
    all_to_all x1, waiting for transfers between devices, on_device(): own = lax.all_to_all(spread, ('za', 'h', 'c'), 0, 0, tiled=True)  16.1 us
    ppermute x8, waiting for transfers between devices, trade(): return lax.ppermute(values, 'y', pairs)  14.2 us
    all_to_all x1, starting transfers between devices, on_device(): lax.all_to_all(picked, ('h', 'par', 'c'), 0, 0, tiled=True)  3.66 us
    pallas_call x1, Pallas kernels, pick(): pl.pallas_call(pick_kernel, out_shape=jax.ShapeDtypeStruct((H, PAR, C, ab...  3.39 us
    pallas_call x1, Pallas kernels, partial_ladder(): pl.pallas_call(ladder_kernel, out_shape=jax.ShapeDtypeStruct((QUAD, owner...  2.48 us
  transfers between devices with their start and end apart: 10, of which 9 were waited for; matrix products, arithmetic and copies ran while one was open for 0% of the time, Pallas kernels for 3%

profile of v3, /device:TPU:1, one launch (start us, length us, event | category | flops | bytes accessed | tf_op | source)
XLA Modules:
  0.0 113.0 jit_solution(2372455887471362263)
XLA Ops:
  0.0 0.8 copy.6
  0.8 0.7 broadcast_in_dim.2
  1.5 20.3 %all-to-all-start = ((bf16[16,8,896]{2,1,0:T(8,128)(2,1)}), bf16[16,8,896]{2,1,0:T(8,128)(2,1)S(1)}, u32[]{:S(2)}, u32[]{:S(2)}) async-start(bf16[16,8,896]{2,1,0:T(8,128)(2,1)} %bitcast.2), calls=%async_computation | async-start | bytes 458752 | tf_op jit(solution)/shard_map/all_to_all | solution.py:159
  21.8 3.4 %pick_blocks.1 = bf16[2,2,2,112,896]{4,3,2,1,0:T(8,128)(2,1)} custom-call(s32[2]{0:T(128)} %irrep_ref.5, bf16[8,112,1792]{2,1,0:T(8,128)(2,1)} %integrals_ref.1), custom_call_target="tpu_custom_call" | custom-call | bytes 2097152 | tf_op jit(solution)/shard_map/pick_blocks/pallas_call | solution.py:47
  25.2 16.1 %all-to-all-done = bf16[16,8,896]{2,1,0:T(8,128)(2,1)S(1)} async-done(((bf16[16,8,896]{2,1,0:T(8,128)(2,1)}), bf16[16,8,896]{2,1,0:T(8,128)(2,1)S(1)}, u32[]{:S(2)}, u32[]{:S(2)}) %all-to-all-start) | async-done | bytes 229408 | tf_op jit(solution)/shard_map/all_to_all | solution.py:159
  41.3 3.7 %all-to-all-start.1 = ((bf16[8,112,896]{2,1,0:T(8,128)(2,1)}), bf16[8,112,896]{2,1,0:T(8,128)(2,1)S(1)}, u32[]{:S(2)}, u32[]{:S(2)}) async-start(bf16[8,112,896]{2,1,0:T(8,128)(2,1)} %bitcast.15), calls=%async_computation.1 | async-start | bytes 3211264 | tf_op jit(solution)/shard_map/all_to_all | solution.py:163
  45.0 5.1 %collective-permute-start.4 = (bf16[1,64,896]{2,1,0:T(8,128)(2,1)S(1)}, bf16[1,64,896]{2,1,0:T(8,128)(2,1)S(1)}, u32[]{:S(2)}, u32[]{:S(2)}) collective-permute-start(bf16[1,64,896]{2,1,0:T(8,128)(2,1)S(1)} %bitcast.19), channel_id=1, source_target_pairs={{0,896},{896,0},{256,128},{128,256},{512,384},{384,512},{768,640},... | collective-permute-start | bytes 344072 | tf_op jit(solution)/shard_map/ppermute | solution.py:20
  50.1 1.9 %collective-permute-start = (bf16[1,64,896]{2,1,0:T(8,128)(2,1)S(1)}, bf16[1,64,896]{2,1,0:T(8,128)(2,1)S(1)}, u32[]{:S(2)}, u32[]{:S(2)}) collective-permute-start(bf16[1,64,896]{2,1,0:T(8,128)(2,1)S(1)} %bitcast.17), channel_id=1, source_target_pairs={{0,128},{128,0},{256,384},{384,256},{512,640},{640,512},{768,896},... | collective-permute-start | bytes 344072 | tf_op jit(solution)/shard_map/ppermute | solution.py:20
  52.1 0.8 collective-permute-done.4
  52.9 2.5 %collective-permute-start.5 = (bf16[2,64,896]{2,1,0:T(8,128)(2,1)S(1)}, bf16[2,64,896]{2,1,0:T(8,128)(2,1)S(1)}, u32[]{:S(2)}, u32[]{:S(2)}) collective-permute-start(bf16[2,64,896]{2,1,0:T(8,128)(2,1)S(1)} %pad_maximum_fusion.1.refs_4_), channel_id=1, source_target_pairs={{0,128},{128,0},{256,384},{384,256},{512,640},{640,512},{768,896},... | collective-permute-start | bytes 688136 | tf_op jit(solution)/shard_map/ppermute | solution.py:20
  55.5 1.5 %collective-permute-done = bf16[1,64,896]{2,1,0:T(8,128)(2,1)S(1)} collective-permute-done((bf16[1,64,896]{2,1,0:T(8,128)(2,1)S(1)}, bf16[1,64,896]{2,1,0:T(8,128)(2,1)S(1)}, u32[]{:S(2)}, u32[]{:S(2)}) %collective-permute-start) | collective-permute-done | bytes 114720 | tf_op jit(solution)/shard_map/ppermute | solution.py:20
  57.0 2.7 %collective-permute-start.1 = (bf16[2,64,896]{2,1,0:T(8,128)(2,1)S(1)}, bf16[2,64,896]{2,1,0:T(8,128)(2,1)S(1)}, u32[]{:S(2)}, u32[]{:S(2)}) collective-permute-start(bf16[2,64,896]{2,1,0:T(8,128)(2,1)S(1)} %pad_maximum_fusion.refs_0_), channel_id=1, source_target_pairs={{0,896},{896,0},{256,128},{128,256},{512,384},{384,512},{768,640},... | collective-permute-start | bytes 688136 | tf_op jit(solution)/shard_map/ppermute | solution.py:20
  59.8 2.4 %collective-permute-done.5.refs_5_ = bf16[2,64,896]{2,1,0:T(8,128)(2,1)S(1)} collective-permute-done((bf16[2,64,896]{2,1,0:T(8,128)(2,1)S(1)}, bf16[2,64,896]{2,1,0:T(8,128)(2,1)S(1)}, u32[]{:S(2)}, u32[]{:S(2)}) %collective-permute-start.5) | collective-permute-done | bytes 229408 | tf_op jit(solution)/shard_map/ppermute | solution.py:20
  62.2 4.6 %collective-permute-start.6 = (bf16[2,64,896]{2,1,0:T(8,128)(2,1)S(1)}, bf16[2,64,896]{2,1,0:T(8,128)(2,1)S(1)}, u32[]{:S(2)}, u32[]{:S(2)}) collective-permute-start(bf16[2,64,896]{2,1,0:T(8,128)(2,1)S(1)} %collective-permute-done.5.refs_5_), channel_id=1, source_target_pairs={{0,896},{896,0},{256,128},{128,256},{512,384},{384,512},{768,640},... | collective-permute-start | bytes 688136 | tf_op jit(solution)/shard_map/ppermute | solution.py:20
  67.2 1.9 %collective-permute-start.2 = (bf16[2,64,896]{2,1,0:T(8,128)(2,1)S(1)}, bf16[2,64,896]{2,1,0:T(8,128)(2,1)S(1)}, u32[]{:S(2)}, u32[]{:S(2)}) collective-permute-start(bf16[2,64,896]{2,1,0:T(8,128)(2,1)S(1)} %collective-permute-done.1.refs_1_), channel_id=1, source_target_pairs={{0,128},{128,0},{256,384},{384,256},{512,640},{640,512},{768,896},... | collective-permute-start | bytes 688136 | tf_op jit(solution)/shard_map/ppermute | solution.py:20
  69.1 2.7 %collective-permute-done.6.refs_6_ = bf16[2,64,896]{2,1,0:T(8,128)(2,1)S(1)} collective-permute-done((bf16[2,64,896]{2,1,0:T(8,128)(2,1)S(1)}, bf16[2,64,896]{2,1,0:T(8,128)(2,1)S(1)}, u32[]{:S(2)}, u32[]{:S(2)}) %collective-permute-start.6) | collective-permute-done | bytes 229408 | tf_op jit(solution)/shard_map/ppermute | solution.py:20
  71.7 2.2 %collective-permute-start.7 = (bf16[2,64,896]{2,1,0:T(8,128)(2,1)S(1)}, bf16[2,64,896]{2,1,0:T(8,128)(2,1)S(1)}, u32[]{:S(2)}, u32[]{:S(2)}) collective-permute-start(bf16[2,64,896]{2,1,0:T(8,128)(2,1)S(1)} %collective-permute-done.6.refs_6_), channel_id=1, source_target_pairs={{0,128},{128,0},{256,384},{384,256},{512,640},{640,512},{768,896},... | collective-permute-start | bytes 688136 | tf_op jit(solution)/shard_map/ppermute | solution.py:20
  74.0 1.2 %collective-permute-done.2.refs_2_ = bf16[2,64,896]{2,1,0:T(8,128)(2,1)S(1)} collective-permute-done((bf16[2,64,896]{2,1,0:T(8,128)(2,1)S(1)}, bf16[2,64,896]{2,1,0:T(8,128)(2,1)S(1)}, u32[]{:S(2)}, u32[]{:S(2)}) %collective-permute-start.2) | collective-permute-done | bytes 229408 | tf_op jit(solution)/shard_map/ppermute | solution.py:20
  75.2 2.8 %collective-permute-start.3 = (bf16[2,64,896]{2,1,0:T(8,128)(2,1)S(1)}, bf16[2,64,896]{2,1,0:T(8,128)(2,1)S(1)}, u32[]{:S(2)}, u32[]{:S(2)}) collective-permute-start(bf16[2,64,896]{2,1,0:T(8,128)(2,1)S(1)} %collective-permute-done.2.refs_2_), channel_id=1, source_target_pairs={{0,896},{896,0},{256,128},{128,256},{512,384},{384,512},{768,640},... | collective-permute-start | bytes 688136 | tf_op jit(solution)/shard_map/ppermute | solution.py:20
  77.9 1.9 %collective-permute-done.7.refs_7_ = bf16[2,64,896]{2,1,0:T(8,128)(2,1)S(1)} collective-permute-done((bf16[2,64,896]{2,1,0:T(8,128)(2,1)S(1)}, bf16[2,64,896]{2,1,0:T(8,128)(2,1)S(1)}, u32[]{:S(2)}, u32[]{:S(2)}) %collective-permute-start.7) | collective-permute-done | bytes 229408 | tf_op jit(solution)/shard_map/ppermute | solution.py:20
  79.8 3.3 %collective-permute-done.3.refs_3_ = bf16[2,64,896]{2,1,0:T(8,128)(2,1)S(1)} collective-permute-done((bf16[2,64,896]{2,1,0:T(8,128)(2,1)S(1)}, bf16[2,64,896]{2,1,0:T(8,128)(2,1)S(1)}, u32[]{:S(2)}, u32[]{:S(2)}) %collective-permute-start.3) | collective-permute-done | bytes 229408 | tf_op jit(solution)/shard_map/ppermute | solution.py:20
  83.1 2.5 %partial_ladder.1 = s16[4,8,64,128]{3,2,1,0:T(8,128)(2,1)S(1)} custom-call(s32[2]{0:T(128)S(1)} %copy-done, s32[8]{0:T(128)S(1)} %copy-done.1, bf16[2,64,896]{2,1,0:T(8,128)(2,1)S(1)} %pad_maximum_fusion.refs_0_, bf16[2,64,896]{2,1,0:T(8,128)(2,1)S(1)} %collective-permute-done.1.refs_1_, bf16[2,64,896]{2,1,0:T(8,128)(2,1)S(1)} %collective-permute-done.2.refs_2_, ...), custom_call_target="tpu_custom_call" | custom-call | flops 822083584 | bytes 6291456 | tf_op jit(solution)/shard_map/partial_ladder/pallas_call | solution.py:136
  85.6 25.2 %all_to_all.15.parts_ref = s16[32,64,128]{2,1,0:T(8,128)(2,1)} all-to-all(s16[32,64,128]{2,1,0:T(8,128)(2,1)S(1)} %bitcast.14), channel_id=1, replica_groups=mesh['y'=8,'za'=4,'h'=2,'par'=2,'x'=4,'c'=2] {'h','par','x','c'}, dimensions={0} | all-to-all | bytes 1048576 | tf_op jit(solution)/shard_map/all_to_all | solution.py:178
  110.8 2.1 %total_ladder.1 = f32[2,112,128]{2,1,0:T(8,128)} custom-call(s32[2]{0:T(128)} %irrep_ref.5, s32[8]{0:T(128)} %fill_ref.3, s16[32,64,128]{2,1,0:T(8,128)(2,1)} %all_to_all.15.parts_ref), custom_call_target="tpu_custom_call" | custom-call | flops 1048576 | bytes 1048576 | tf_op jit(solution)/shard_map/total_ladder/pallas_call | solution.py:121
  (9 shorter events, 0.5 us)
Async XLA Ops:
  1.5 39.8 %all-to-all-start = ((bf16[16,8,896]{2,1,0:T(8,128)(2,1)}), bf16[16,8,896]{2,1,0:T(8,128)(2,1)S(1)}, u32[]{:S(2)}, u32[]{:S(2)}) async-start(bf16[16,8,896]{2,1,0:T(8,128)(2,1)} %bitcast.2), calls=%async_computation | async-start | bytes 458752 | tf_op jit(solution)/shard_map/all_to_all | solution.py:159
  41.3 41.8 %copy-start = (s32[2]{0:T(128)S(1)}, s32[2]{0:T(128)}, u32[]{:S(2)}) copy-start(s32[2]{0:T(128)} %irrep_ref.5) | copy-start | bytes 28
  41.3 41.8 %copy-start.1 = (s32[8]{0:T(128)S(1)}, s32[8]{0:T(128)}, u32[]{:S(2)}) copy-start(s32[8]{0:T(128)} %fill_ref.3) | copy-start | bytes 100
  41.3 41.8 %all-to-all-start.1 = ((bf16[8,112,896]{2,1,0:T(8,128)(2,1)}), bf16[8,112,896]{2,1,0:T(8,128)(2,1)S(1)}, u32[]{:S(2)}, u32[]{:S(2)}) async-start(bf16[8,112,896]{2,1,0:T(8,128)(2,1)} %bitcast.15), calls=%async_computation.1 | async-start | bytes 3211264 | tf_op jit(solution)/shard_map/all_to_all | solution.py:163
  45.0 7.9 %collective-permute-start.4 = (bf16[1,64,896]{2,1,0:T(8,128)(2,1)S(1)}, bf16[1,64,896]{2,1,0:T(8,128)(2,1)S(1)}, u32[]{:S(2)}, u32[]{:S(2)}) collective-permute-start(bf16[1,64,896]{2,1,0:T(8,128)(2,1)S(1)} %bitcast.19), channel_id=1, source_target_pairs={{0,896},{896,0},{256,128},{128,256},{512,384},{384,512},{768,640},... | collective-permute-start | bytes 344072 | tf_op jit(solution)/shard_map/ppermute | solution.py:20
  50.1 6.9 %collective-permute-start = (bf16[1,64,896]{2,1,0:T(8,128)(2,1)S(1)}, bf16[1,64,896]{2,1,0:T(8,128)(2,1)S(1)}, u32[]{:S(2)}, u32[]{:S(2)}) collective-permute-start(bf16[1,64,896]{2,1,0:T(8,128)(2,1)S(1)} %bitcast.17), channel_id=1, source_target_pairs={{0,128},{128,0},{256,384},{384,256},{512,640},{640,512},{768,896},... | collective-permute-start | bytes 344072 | tf_op jit(solution)/shard_map/ppermute | solution.py:20
  52.9 9.2 %collective-permute-start.5 = (bf16[2,64,896]{2,1,0:T(8,128)(2,1)S(1)}, bf16[2,64,896]{2,1,0:T(8,128)(2,1)S(1)}, u32[]{:S(2)}, u32[]{:S(2)}) collective-permute-start(bf16[2,64,896]{2,1,0:T(8,128)(2,1)S(1)} %pad_maximum_fusion.1.refs_4_), channel_id=1, source_target_pairs={{0,128},{128,0},{256,384},{384,256},{512,640},{640,512},{768,896},... | collective-permute-start | bytes 688136 | tf_op jit(solution)/shard_map/ppermute | solution.py:20
  57.0 10.1 %collective-permute-start.1 = (bf16[2,64,896]{2,1,0:T(8,128)(2,1)S(1)}, bf16[2,64,896]{2,1,0:T(8,128)(2,1)S(1)}, u32[]{:S(2)}, u32[]{:S(2)}) collective-permute-start(bf16[2,64,896]{2,1,0:T(8,128)(2,1)S(1)} %pad_maximum_fusion.refs_0_), channel_id=1, source_target_pairs={{0,896},{896,0},{256,128},{128,256},{512,384},{384,512},{768,640},... | collective-permute-start | bytes 688136 | tf_op jit(solution)/shard_map/ppermute | solution.py:20
  62.2 9.6 %collective-permute-start.6 = (bf16[2,64,896]{2,1,0:T(8,128)(2,1)S(1)}, bf16[2,64,896]{2,1,0:T(8,128)(2,1)S(1)}, u32[]{:S(2)}, u32[]{:S(2)}) collective-permute-start(bf16[2,64,896]{2,1,0:T(8,128)(2,1)S(1)} %collective-permute-done.5.refs_5_), channel_id=1, source_target_pairs={{0,896},{896,0},{256,128},{128,256},{512,384},{384,512},{768,640},... | collective-permute-start | bytes 688136 | tf_op jit(solution)/shard_map/ppermute | solution.py:20
  67.2 8.0 %collective-permute-start.2 = (bf16[2,64,896]{2,1,0:T(8,128)(2,1)S(1)}, bf16[2,64,896]{2,1,0:T(8,128)(2,1)S(1)}, u32[]{:S(2)}, u32[]{:S(2)}) collective-permute-start(bf16[2,64,896]{2,1,0:T(8,128)(2,1)S(1)} %collective-permute-done.1.refs_1_), channel_id=1, source_target_pairs={{0,128},{128,0},{256,384},{384,256},{512,640},{640,512},{768,896},... | collective-permute-start | bytes 688136 | tf_op jit(solution)/shard_map/ppermute | solution.py:20
  71.7 8.1 %collective-permute-start.7 = (bf16[2,64,896]{2,1,0:T(8,128)(2,1)S(1)}, bf16[2,64,896]{2,1,0:T(8,128)(2,1)S(1)}, u32[]{:S(2)}, u32[]{:S(2)}) collective-permute-start(bf16[2,64,896]{2,1,0:T(8,128)(2,1)S(1)} %collective-permute-done.6.refs_6_), channel_id=1, source_target_pairs={{0,128},{128,0},{256,384},{384,256},{512,640},{640,512},{768,896},... | collective-permute-start | bytes 688136 | tf_op jit(solution)/shard_map/ppermute | solution.py:20
  75.2 8.0 %collective-permute-start.3 = (bf16[2,64,896]{2,1,0:T(8,128)(2,1)S(1)}, bf16[2,64,896]{2,1,0:T(8,128)(2,1)S(1)}, u32[]{:S(2)}, u32[]{:S(2)}) collective-permute-start(bf16[2,64,896]{2,1,0:T(8,128)(2,1)S(1)} %collective-permute-done.2.refs_2_), channel_id=1, source_target_pairs={{0,896},{896,0},{256,128},{128,256},{512,384},{384,512},{768,640},... | collective-permute-start | bytes 688136 | tf_op jit(solution)/shard_map/ppermute | solution.py:20

commit v4 on v3

--- a/solution.py
+++ b/solution.py
@@ -55,24 +55,43 @@
     )(batch_irrep, integrals)
 
 
-def ladder_kernel(irrep_ref, fill_ref, *refs):
-    pairs, blocks_ref = refs[: 4 * C], refs[4 * C]
-    out_ref, left, right = refs[4 * C + 1 :]
+def used_columns(irrep_ref, fill_ref, part, cols):
+    x, h, core = (lax.axis_index(axis) for axis in ("x", "h", "c"))
+    place = ((x * C + part) * H + h) * cols + lax.broadcasted_iota(jnp.int32, (1, cols), 1)
+    return place < fill_ref[irrep_ref[core]]
+
+
+def as_integers(tile, ab_rows):
+    column = lax.broadcasted_iota(jnp.int32, (1, LANES), 1)
+    peak = jnp.max(jnp.abs(tile), axis=1, keepdims=True)
+    power = jnp.clip(jnp.ceil(jnp.log2(jnp.maximum(peak * 1.0001, 1e-37))), -111.0, 111.0)
+    scaled = jnp.where(column == ab_rows, power, tile * jnp.exp2(TOP - power))
+    return jnp.floor(scaled + 0.5).astype(jnp.int32).astype(jnp.int16)
+
+
+def inside_block(tile, ab_rows):
+    column = lax.broadcasted_iota(jnp.int32, (1, LANES), 1)
+    return jnp.where(column < ab_rows, tile, jnp.zeros((), jnp.float32))
+
+
+def early_kernel(irrep_ref, fill_ref, *refs):
+    pairs, blocks_ref = refs[: 4 * C - 1], refs[4 * C - 1]
+    out_ref, open_ref, left, right, held = refs[4 * C :]
     _, rows, cols = pairs[0].shape
     parts, ab_rows = blocks_ref.shape[1:3]
-    y, x, h, core = (lax.axis_index(axis) for axis in ("y", "x", "h", "c"))
-
-    limit = fill_ref[irrep_ref[core]]
+    y = lax.axis_index("y")
     for part in range(parts):
-        place = ((x * C + part) * H + h) * cols + lax.broadcasted_iota(jnp.int32, (1, cols), 1)
-        used = place < limit
+        used = used_columns(irrep_ref, fill_ref, part, cols)
         for at in range(Y):
-            values = pairs[part * 4 + at // 2][at % 2]
-            left[part, owner_of(y, part, at)] = jnp.where(used, values, jnp.zeros((), values.dtype))
+            owner = owner_of(y, part, at)
+            if part == 0 and at >= Y - 2:
+                left[part, owner] = jnp.zeros((rows, cols), left.dtype)
+            else:
+                values = (pairs[:3] if part == 0 else pairs[3:])[at // 2][at % 2]
+                left[part, owner] = jnp.where(used, values, jnp.zeros((), values.dtype))
     for at in range(QUAD):
         for part in range(parts):
             right[part, at, pl.ds(0, ab_rows)] = blocks_ref[at, part]
-    column = lax.broadcasted_iota(jnp.int32, (1, LANES), 1)
     for half in range(QUAD // 2):
         product = sum(
             lax.dot_general(
@@ -84,13 +103,66 @@
             for part in range(parts)
         )
         for side in range(2):
-            tile = product[:, side * LANES : (side + 1) * LANES]
-            tile = jnp.where(column < ab_rows, tile, jnp.zeros((), jnp.float32))
-            peak = jnp.max(jnp.abs(tile), axis=1, keepdims=True)
-            power = jnp.clip(jnp.ceil(jnp.log2(jnp.maximum(peak * 1.0001, 1e-37))), -111.0, 111.0)
-            scaled = jnp.where(column == ab_rows, power, tile * jnp.exp2(TOP - power))
-            whole = jnp.floor(scaled + 0.5).astype(jnp.int32).astype(jnp.int16)
-            out_ref[2 * half + side] = whole.reshape(Y, rows, LANES)
+            tile = inside_block(product[:, side * LANES : (side + 1) * LANES], ab_rows)
+            held[...] = tile.reshape(Y, rows, LANES)
+            for late in range(2):
+                open_ref[2 * half + side, late] = held[owner_of(y, 0, Y - 2 + late)]
+            out_ref[2 * half + side] = as_integers(tile, ab_rows).reshape(Y, rows, LANES)
+
+
+def late_kernel(irrep_ref, fill_ref, last_ref, blocks_ref, early_ref, open_ref, out_ref, right):
+    _, rows, cols = last_ref.shape
+    ab_rows = blocks_ref.shape[2]
+    y = lax.axis_index("y")
+    values = last_ref[...].reshape(2 * rows, cols)
+    used = used_columns(irrep_ref, fill_ref, 0, cols)
+    values = jnp.where(used, values, jnp.zeros((), values.dtype))
+    for at in range(QUAD):
+        right[at, pl.ds(0, ab_rows)] = blocks_ref[at, 0]
+    out_ref[...] = early_ref[...]
+    for half in range(QUAD // 2):
+        product = lax.dot_general(
+            values,
+            right[pl.ds(2 * half, 2)].reshape(2 * LANES, cols),
+            (((1,), (1,)), ((), ())),
+            preferred_element_type=jnp.float32,
+        )
+        for side in range(2):
+            tile = inside_block(product[:, side * LANES : (side + 1) * LANES], ab_rows)
+            for late in range(2):
+                whole = tile[late * rows : (late + 1) * rows] + open_ref[2 * half + side, late]
+                out_ref[2 * half + side, owner_of(y, 0, Y - 2 + late)] = as_integers(whole, ab_rows)
+
+
+def partial_ladder(batch_irrep, pair_fill, pairs, blocks):
+    _, rows, cols = pairs[0].shape
+    parts, ab_rows = blocks.shape[1:3]
+    smem, vmem = pl.BlockSpec(memory_space=pltpu.SMEM), pl.BlockSpec(memory_space=pltpu.VMEM)
+    whole = jax.ShapeDtypeStruct((QUAD, Y, rows, LANES), jnp.int16)
+    early, still_open = pl.pallas_call(
+        early_kernel,
+        out_shape=(whole, jax.ShapeDtypeStruct((QUAD, 2, rows, LANES), jnp.float32)),
+        in_specs=[smem] * 2 + [vmem] * len(pairs),
+        out_specs=[vmem] * 2,
+        scratch_shapes=[
+            pltpu.VMEM((parts, Y, rows, cols), jnp.bfloat16),
+            pltpu.VMEM((parts, QUAD, LANES, cols), jnp.bfloat16),
+            pltpu.VMEM((Y, rows, LANES), jnp.float32),
+        ],
+        compiler_params=pltpu.CompilerParams(vmem_limit_bytes=24 * 2**20),
+        cost_estimate=pl.CostEstimate(flops=2**30, bytes_accessed=6 * 2**20, transcendentals=0),
+        name="early_ladder",
+    )(batch_irrep, pair_fill, *pairs[:3], *pairs[4:], blocks)
+    return pl.pallas_call(
+        late_kernel,
+        out_shape=whole,
+        in_specs=[smem] * 2 + [vmem] * 4,
+        out_specs=vmem,
+        scratch_shapes=[pltpu.VMEM((QUAD, LANES, cols), jnp.bfloat16)],
+        compiler_params=pltpu.CompilerParams(vmem_limit_bytes=24 * 2**20),
+        cost_estimate=pl.CostEstimate(flops=2**28, bytes_accessed=2 * 2**20, transcendentals=0),
+        name="late_ladder",
+    )(batch_irrep, pair_fill, pairs[3], blocks, early, still_open)
 
 
 def total_kernel(irrep_ref, fill_ref, parts_ref, out_ref):
@@ -128,27 +200,6 @@
     )(batch_irrep, pair_fill, parts)
 
 
-def partial_ladder(batch_irrep, pair_fill, pairs, blocks):
-    _, rows, cols = pairs[0].shape
-    parts, ab_rows = blocks.shape[1:3]
-    owners = Y
-    flops = 2 * owners * rows * QUAD * ab_rows * parts * cols
-    return pl.pallas_call(
-        ladder_kernel,
-        out_shape=jax.ShapeDtypeStruct((QUAD, owners, rows, LANES), jnp.int16),
-        in_specs=[pl.BlockSpec(memory_space=pltpu.SMEM)] * 2
-        + [pl.BlockSpec(memory_space=pltpu.VMEM)] * (len(pairs) + 1),
-        out_specs=pl.BlockSpec(memory_space=pltpu.VMEM),
-        scratch_shapes=[
-            pltpu.VMEM((parts, owners, rows, cols), jnp.bfloat16),
-            pltpu.VMEM((parts, QUAD, LANES, cols), jnp.bfloat16),
-        ],
-        compiler_params=pltpu.CompilerParams(vmem_limit_bytes=24 * 2**20),
-        cost_estimate=pl.CostEstimate(flops=flops, bytes_accessed=6 * 2**20, transcendentals=0),
-        name="partial_ladder",
-    )(batch_irrep, pair_fill, *pairs, blocks)
-
-
 def on_device(amplitudes, integrals, batch_irrep, pair_fill):
     batches, own_pairs, cd_cols = amplitudes.shape
     ab_rows = integrals.shape[1]

time: 114 us -> 112 us (0.982)
  waiting for transfers between devices: 30.3 us -> 28.9 us
  Pallas kernels: 8.01 us -> 9.23 us
    ppermute x8, waiting for transfers between devices: 14.2 us -> 10.9 us  [trade(): return lax.ppermute(values, 'y', pairs)]
    all_to_all x1, waiting for transfers between devices: 0.01 us -> 1.9 us  [on_device(): lax.all_to_all(picked, ('h', 'par', 'c'), 0, 0, tiled=True)]
    pallas_call x1 -> x2, Pallas kernels: 2.48 us -> 3.7 us  [the longest x1 2.53 us: partial_ladder(): pl.pallas_call(early_kernel, out_shape=(whole, jax.ShapeDtypeStruct((QUAD...]
    all_to_all x1, blocking collectives: 25.2 us -> 24.1 us  [on_device(): parts = lax.all_to_all(partial, ('h', 'par', 'x', 'c'), 0, 0, tiled=True)]
  transfers between devices with their start and end apart: 10 -> 10, of which waited for: 9 -> 9; matrix products, arithmetic and copies ran while one was open for 0% -> 0% of each run, Pallas kernels for 3% -> 5%
where the time goes in v4:
time: 112 us
  starting transfers between devices  47.7 us (43%)
  waiting for transfers between devices  28.9 us (26%)
  blocking collectives  24.1 us (22%)
  Pallas kernels  9.23 us (8%)
  local copies, waits for them, and re-layouts  1.57 us (1%)
    all_to_all x1, blocking collectives, on_device(): parts = lax.all_to_all(partial, ('h', 'par', 'x', 'c'), 0, 0, tiled=True)  24.1 us
    ppermute x8, starting transfers between devices, trade(): return lax.ppermute(values, 'y', pairs)  23.8 us
    all_to_all x1, starting transfers between devices, on_device(): own = lax.all_to_all(spread, ('za', 'h', 'c'), 0, 0, tiled=True)  20.3 us
    all_to_all x1, waiting for transfers between devices, on_device(): own = lax.all_to_all(spread, ('za', 'h', 'c'), 0, 0, tiled=True)  16.1 us
    ppermute x8, waiting for transfers between devices, trade(): return lax.ppermute(values, 'y', pairs)  10.9 us
    all_to_all x1, starting transfers between devices, on_device(): lax.all_to_all(picked, ('h', 'par', 'c'), 0, 0, tiled=True)  3.66 us
    pallas_call x1, Pallas kernels, pick(): pl.pallas_call(pick_kernel, out_shape=jax.ShapeDtypeStruct((H, PAR, C, ab...  3.38 us
    pallas_call x1, Pallas kernels, partial_ladder(): pl.pallas_call(early_kernel, out_shape=(whole, jax.ShapeDtypeStruct((QUAD...  2.53 us
  transfers between devices with their start and end apart: 10, of which 9 were waited for; matrix products, arithmetic and copies ran while one was open for 0% of the time, Pallas kernels for 5%

profile of v4, /device:TPU:1, one launch (start us, length us, event | category | flops | bytes accessed | tf_op | source)
XLA Modules:
  0.0 111.7 jit_solution(5399796099495990657)
XLA Ops:
  0.0 0.8 copy.6
  1.5 20.3 %all-to-all-start = ((bf16[16,8,896]{2,1,0:T(8,128)(2,1)}), bf16[16,8,896]{2,1,0:T(8,128)(2,1)S(1)}, u32[]{:S(2)}, u32[]{:S(2)}) async-start(bf16[16,8,896]{2,1,0:T(8,128)(2,1)} %bitcast.2), calls=%async_computation | async-start | bytes 458752 | tf_op jit(solution)/shard_map/all_to_all | solution.py:210
  21.8 3.4 %pick_blocks.1 = bf16[2,2,2,112,896]{4,3,2,1,0:T(8,128)(2,1)} custom-call(s32[2]{0:T(128)} %irrep_ref.7, bf16[8,112,1792]{2,1,0:T(8,128)(2,1)} %integrals_ref.1), custom_call_target="tpu_custom_call" | custom-call | bytes 2097152 | tf_op jit(solution)/shard_map/pick_blocks/pallas_call | solution.py:47
  25.2 16.1 %all-to-all-done = bf16[16,8,896]{2,1,0:T(8,128)(2,1)S(1)} async-done(((bf16[16,8,896]{2,1,0:T(8,128)(2,1)}), bf16[16,8,896]{2,1,0:T(8,128)(2,1)S(1)}, u32[]{:S(2)}, u32[]{:S(2)}) %all-to-all-start) | async-done | bytes 229408 | tf_op jit(solution)/shard_map/all_to_all | solution.py:210
  41.3 3.7 %all-to-all-start.1 = ((bf16[8,112,896]{2,1,0:T(8,128)(2,1)}), bf16[8,112,896]{2,1,0:T(8,128)(2,1)S(1)}, u32[]{:S(2)}, u32[]{:S(2)}) async-start(bf16[8,112,896]{2,1,0:T(8,128)(2,1)} %bitcast.16), calls=%async_computation.1 | async-start | bytes 3211264 | tf_op jit(solution)/shard_map/all_to_all | solution.py:214
  45.0 5.1 %collective-permute-start.4 = (bf16[1,64,896]{2,1,0:T(8,128)(2,1)S(1)}, bf16[1,64,896]{2,1,0:T(8,128)(2,1)S(1)}, u32[]{:S(2)}, u32[]{:S(2)}) collective-permute-start(bf16[1,64,896]{2,1,0:T(8,128)(2,1)S(1)} %bitcast.20), channel_id=1, source_target_pairs={{0,896},{896,0},{256,128},{128,256},{512,384},{384,512},{768,640},... | collective-permute-start | bytes 344072 | tf_op jit(solution)/shard_map/ppermute | solution.py:20
  50.1 1.9 %collective-permute-start = (bf16[1,64,896]{2,1,0:T(8,128)(2,1)S(1)}, bf16[1,64,896]{2,1,0:T(8,128)(2,1)S(1)}, u32[]{:S(2)}, u32[]{:S(2)}) collective-permute-start(bf16[1,64,896]{2,1,0:T(8,128)(2,1)S(1)} %bitcast.18), channel_id=1, source_target_pairs={{0,128},{128,0},{256,384},{384,256},{512,640},{640,512},{768,896},... | collective-permute-start | bytes 344072 | tf_op jit(solution)/shard_map/ppermute | solution.py:20
  52.1 0.8 collective-permute-done.4
  52.9 2.5 %collective-permute-start.5 = (bf16[2,64,896]{2,1,0:T(8,128)(2,1)S(1)}, bf16[2,64,896]{2,1,0:T(8,128)(2,1)S(1)}, u32[]{:S(2)}, u32[]{:S(2)}) collective-permute-start(bf16[2,64,896]{2,1,0:T(8,128)(2,1)S(1)} %pad_maximum_fusion.1.refs_3_), channel_id=1, source_target_pairs={{0,128},{128,0},{256,384},{384,256},{512,640},{640,512},{768,896},... | collective-permute-start | bytes 688136 | tf_op jit(solution)/shard_map/ppermute | solution.py:20
  55.5 1.5 %collective-permute-done = bf16[1,64,896]{2,1,0:T(8,128)(2,1)S(1)} collective-permute-done((bf16[1,64,896]{2,1,0:T(8,128)(2,1)S(1)}, bf16[1,64,896]{2,1,0:T(8,128)(2,1)S(1)}, u32[]{:S(2)}, u32[]{:S(2)}) %collective-permute-start) | collective-permute-done | bytes 114720 | tf_op jit(solution)/shard_map/ppermute | solution.py:20
  57.0 2.7 %collective-permute-start.1 = (bf16[2,64,896]{2,1,0:T(8,128)(2,1)S(1)}, bf16[2,64,896]{2,1,0:T(8,128)(2,1)S(1)}, u32[]{:S(2)}, u32[]{:S(2)}) collective-permute-start(bf16[2,64,896]{2,1,0:T(8,128)(2,1)S(1)} %pad_maximum_fusion.refs_0_), channel_id=1, source_target_pairs={{0,896},{896,0},{256,128},{128,256},{512,384},{384,512},{768,640},... | collective-permute-start | bytes 688136 | tf_op jit(solution)/shard_map/ppermute | solution.py:20
  59.8 2.4 %collective-permute-done.5.refs_4_ = bf16[2,64,896]{2,1,0:T(8,128)(2,1)S(1)} collective-permute-done((bf16[2,64,896]{2,1,0:T(8,128)(2,1)S(1)}, bf16[2,64,896]{2,1,0:T(8,128)(2,1)S(1)}, u32[]{:S(2)}, u32[]{:S(2)}) %collective-permute-start.5) | collective-permute-done | bytes 229408 | tf_op jit(solution)/shard_map/ppermute | solution.py:20
  62.2 4.6 %collective-permute-start.6 = (bf16[2,64,896]{2,1,0:T(8,128)(2,1)S(1)}, bf16[2,64,896]{2,1,0:T(8,128)(2,1)S(1)}, u32[]{:S(2)}, u32[]{:S(2)}) collective-permute-start(bf16[2,64,896]{2,1,0:T(8,128)(2,1)S(1)} %collective-permute-done.5.refs_4_), channel_id=1, source_target_pairs={{0,896},{896,0},{256,128},{128,256},{512,384},{384,512},{768,640},... | collective-permute-start | bytes 688136 | tf_op jit(solution)/shard_map/ppermute | solution.py:20
  67.2 1.9 %collective-permute-start.2 = (bf16[2,64,896]{2,1,0:T(8,128)(2,1)S(1)}, bf16[2,64,896]{2,1,0:T(8,128)(2,1)S(1)}, u32[]{:S(2)}, u32[]{:S(2)}) collective-permute-start(bf16[2,64,896]{2,1,0:T(8,128)(2,1)S(1)} %collective-permute-done.1.refs_1_), channel_id=1, source_target_pairs={{0,128},{128,0},{256,384},{384,256},{512,640},{640,512},{768,896},... | collective-permute-start | bytes 688136 | tf_op jit(solution)/shard_map/ppermute | solution.py:20
  69.1 2.7 %collective-permute-done.6.refs_5_ = bf16[2,64,896]{2,1,0:T(8,128)(2,1)S(1)} collective-permute-done((bf16[2,64,896]{2,1,0:T(8,128)(2,1)S(1)}, bf16[2,64,896]{2,1,0:T(8,128)(2,1)S(1)}, u32[]{:S(2)}, u32[]{:S(2)}) %collective-permute-start.6) | collective-permute-done | bytes 229408 | tf_op jit(solution)/shard_map/ppermute | solution.py:20
  71.7 2.2 %collective-permute-start.7 = (bf16[2,64,896]{2,1,0:T(8,128)(2,1)S(1)}, bf16[2,64,896]{2,1,0:T(8,128)(2,1)S(1)}, u32[]{:S(2)}, u32[]{:S(2)}) collective-permute-start(bf16[2,64,896]{2,1,0:T(8,128)(2,1)S(1)} %collective-permute-done.6.refs_5_), channel_id=1, source_target_pairs={{0,128},{128,0},{256,384},{384,256},{512,640},{640,512},{768,896},... | collective-permute-start | bytes 688136 | tf_op jit(solution)/shard_map/ppermute | solution.py:20
  74.0 1.2 %collective-permute-done.2.refs_2_ = bf16[2,64,896]{2,1,0:T(8,128)(2,1)S(1)} collective-permute-done((bf16[2,64,896]{2,1,0:T(8,128)(2,1)S(1)}, bf16[2,64,896]{2,1,0:T(8,128)(2,1)S(1)}, u32[]{:S(2)}, u32[]{:S(2)}) %collective-permute-start.2) | collective-permute-done | bytes 229408 | tf_op jit(solution)/shard_map/ppermute | solution.py:20
  75.1 2.8 %collective-permute-start.3 = (bf16[2,64,896]{2,1,0:T(8,128)(2,1)S(1)}, bf16[2,64,896]{2,1,0:T(8,128)(2,1)S(1)}, u32[]{:S(2)}, u32[]{:S(2)}) collective-permute-start(bf16[2,64,896]{2,1,0:T(8,128)(2,1)S(1)} %collective-permute-done.2.refs_2_), channel_id=1, source_target_pairs={{0,896},{896,0},{256,128},{128,256},{512,384},{384,512},{768,640},... | collective-permute-start | bytes 688136 | tf_op jit(solution)/shard_map/ppermute | solution.py:20
  77.9 1.9 %collective-permute-done.7.refs_6_ = bf16[2,64,896]{2,1,0:T(8,128)(2,1)S(1)} collective-permute-done((bf16[2,64,896]{2,1,0:T(8,128)(2,1)S(1)}, bf16[2,64,896]{2,1,0:T(8,128)(2,1)S(1)}, u32[]{:S(2)}, u32[]{:S(2)}) %collective-permute-start.7) | collective-permute-done | bytes 229408 | tf_op jit(solution)/shard_map/ppermute | solution.py:20
  79.8 1.9 %all-to-all-done.1 = bf16[8,112,896]{2,1,0:T(8,128)(2,1)S(1)} async-done(((bf16[8,112,896]{2,1,0:T(8,128)(2,1)}), bf16[8,112,896]{2,1,0:T(8,128)(2,1)S(1)}, u32[]{:S(2)}, u32[]{:S(2)}) %all-to-all-start.1) | async-done | bytes 1605664 | tf_op jit(solution)/shard_map/all_to_all | solution.py:214
  81.7 2.5 %early_ladder.1 = (s16[4,8,64,128]{3,2,1,0:T(8,128)(2,1)S(1)}, f32[4,2,64,128]{3,2,1,0:T(8,128)S(1)}) custom-call(s32[2]{0:T(128)S(1)} %copy-done, s32[8]{0:T(128)S(1)} %copy-done.1, bf16[2,64,896]{2,1,0:T(8,128)(2,1)S(1)} %pad_maximum_fusion.refs_0_, bf16[2,64,896]{2,1,0:T(8,128)(2,1)S(1)} %collective-permute-done.1.refs_1_, ...), custom_call_target="tpu_custom_call" | custom-call | flops 1073741824 | bytes 6291456 | tf_op jit(solution)/shard_map/early_ladder/pallas_call | solution.py:142
  84.3 1.2 %late_ladder.1 = s16[4,8,64,128]{3,2,1,0:T(8,128)(2,1)S(1)} custom-call(s32[2]{0:T(128)S(1)} %copy-done, s32[8]{0:T(128)S(1)} %copy-done.1, bf16[2,64,896]{2,1,0:T(8,128)(2,1)S(1)} %collective-permute-done.3.last_ref, bf16[4,2,112,896]{3,2,1,0:T(8,128)(2,1)S(1)} %bitcast.14, s16[4,8,64,128]{3,2,1,0:T(8,128)(2,1)S(1)} %get-tuple-element.7.early_ref, ...), custom_call_target="tpu_custom_call" | custom-call | flops 268435456 | bytes 2097152 | tf_op jit(solution)/shard_map/late_ladder/pallas_call | solution.py:156
  85.5 24.1 %all_to_all.15.parts_ref = s16[32,64,128]{2,1,0:T(8,128)(2,1)} all-to-all(s16[32,64,128]{2,1,0:T(8,128)(2,1)S(1)} %bitcast.15), channel_id=1, replica_groups=mesh['y'=8,'za'=4,'h'=2,'par'=2,'x'=4,'c'=2] {'h','par','x','c'}, dimensions={0} | all-to-all | bytes 1048576 | tf_op jit(solution)/shard_map/all_to_all | solution.py:229
  109.5 2.1 %total_ladder.1 = f32[2,112,128]{2,1,0:T(8,128)} custom-call(s32[2]{0:T(128)} %irrep_ref.7, s32[8]{0:T(128)} %fill_ref.5, s16[32,64,128]{2,1,0:T(8,128)(2,1)} %all_to_all.15.parts_ref), custom_call_target="tpu_custom_call" | custom-call | flops 1048576 | bytes 1048576 | tf_op jit(solution)/shard_map/total_ladder/pallas_call | solution.py:193
  (10 shorter events, 1.2 us)
Async XLA Ops:
  1.5 39.8 %all-to-all-start = ((bf16[16,8,896]{2,1,0:T(8,128)(2,1)}), bf16[16,8,896]{2,1,0:T(8,128)(2,1)S(1)}, u32[]{:S(2)}, u32[]{:S(2)}) async-start(bf16[16,8,896]{2,1,0:T(8,128)(2,1)} %bitcast.2), calls=%async_computation | async-start | bytes 458752 | tf_op jit(solution)/shard_map/all_to_all | solution.py:210
  41.3 40.4 %copy-start = (s32[2]{0:T(128)S(1)}, s32[2]{0:T(128)}, u32[]{:S(2)}) copy-start(s32[2]{0:T(128)} %irrep_ref.7) | copy-start | bytes 28
  41.3 40.4 %copy-start.1 = (s32[8]{0:T(128)S(1)}, s32[8]{0:T(128)}, u32[]{:S(2)}) copy-start(s32[8]{0:T(128)} %fill_ref.5) | copy-start | bytes 100
  41.3 40.4 %all-to-all-start.1 = ((bf16[8,112,896]{2,1,0:T(8,128)(2,1)}), bf16[8,112,896]{2,1,0:T(8,128)(2,1)S(1)}, u32[]{:S(2)}, u32[]{:S(2)}) async-start(bf16[8,112,896]{2,1,0:T(8,128)(2,1)} %bitcast.16), calls=%async_computation.1 | async-start | bytes 3211264 | tf_op jit(solution)/shard_map/all_to_all | solution.py:214
  45.0 7.9 %collective-permute-start.4 = (bf16[1,64,896]{2,1,0:T(8,128)(2,1)S(1)}, bf16[1,64,896]{2,1,0:T(8,128)(2,1)S(1)}, u32[]{:S(2)}, u32[]{:S(2)}) collective-permute-start(bf16[1,64,896]{2,1,0:T(8,128)(2,1)S(1)} %bitcast.20), channel_id=1, source_target_pairs={{0,896},{896,0},{256,128},{128,256},{512,384},{384,512},{768,640},... | collective-permute-start | bytes 344072 | tf_op jit(solution)/shard_map/ppermute | solution.py:20
  50.1 6.9 %collective-permute-start = (bf16[1,64,896]{2,1,0:T(8,128)(2,1)S(1)}, bf16[1,64,896]{2,1,0:T(8,128)(2,1)S(1)}, u32[]{:S(2)}, u32[]{:S(2)}) collective-permute-start(bf16[1,64,896]{2,1,0:T(8,128)(2,1)S(1)} %bitcast.18), channel_id=1, source_target_pairs={{0,128},{128,0},{256,384},{384,256},{512,640},{640,512},{768,896},... | collective-permute-start | bytes 344072 | tf_op jit(solution)/shard_map/ppermute | solution.py:20
  52.9 9.2 %collective-permute-start.5 = (bf16[2,64,896]{2,1,0:T(8,128)(2,1)S(1)}, bf16[2,64,896]{2,1,0:T(8,128)(2,1)S(1)}, u32[]{:S(2)}, u32[]{:S(2)}) collective-permute-start(bf16[2,64,896]{2,1,0:T(8,128)(2,1)S(1)} %pad_maximum_fusion.1.refs_3_), channel_id=1, source_target_pairs={{0,128},{128,0},{256,384},{384,256},{512,640},{640,512},{768,896},... | collective-permute-start | bytes 688136 | tf_op jit(solution)/shard_map/ppermute | solution.py:20
  57.0 10.1 %collective-permute-start.1 = (bf16[2,64,896]{2,1,0:T(8,128)(2,1)S(1)}, bf16[2,64,896]{2,1,0:T(8,128)(2,1)S(1)}, u32[]{:S(2)}, u32[]{:S(2)}) collective-permute-start(bf16[2,64,896]{2,1,0:T(8,128)(2,1)S(1)} %pad_maximum_fusion.refs_0_), channel_id=1, source_target_pairs={{0,896},{896,0},{256,128},{128,256},{512,384},{384,512},{768,640},... | collective-permute-start | bytes 688136 | tf_op jit(solution)/shard_map/ppermute | solution.py:20
  62.2 9.6 %collective-permute-start.6 = (bf16[2,64,896]{2,1,0:T(8,128)(2,1)S(1)}, bf16[2,64,896]{2,1,0:T(8,128)(2,1)S(1)}, u32[]{:S(2)}, u32[]{:S(2)}) collective-permute-start(bf16[2,64,896]{2,1,0:T(8,128)(2,1)S(1)} %collective-permute-done.5.refs_4_), channel_id=1, source_target_pairs={{0,896},{896,0},{256,128},{128,256},{512,384},{384,512},{768,640},... | collective-permute-start | bytes 688136 | tf_op jit(solution)/shard_map/ppermute | solution.py:20
  67.2 8.0 %collective-permute-start.2 = (bf16[2,64,896]{2,1,0:T(8,128)(2,1)S(1)}, bf16[2,64,896]{2,1,0:T(8,128)(2,1)S(1)}, u32[]{:S(2)}, u32[]{:S(2)}) collective-permute-start(bf16[2,64,896]{2,1,0:T(8,128)(2,1)S(1)} %collective-permute-done.1.refs_1_), channel_id=1, source_target_pairs={{0,128},{128,0},{256,384},{384,256},{512,640},{640,512},{768,896},... | collective-permute-start | bytes 688136 | tf_op jit(solution)/shard_map/ppermute | solution.py:20
  71.7 8.1 %collective-permute-start.7 = (bf16[2,64,896]{2,1,0:T(8,128)(2,1)S(1)}, bf16[2,64,896]{2,1,0:T(8,128)(2,1)S(1)}, u32[]{:S(2)}, u32[]{:S(2)}) collective-permute-start(bf16[2,64,896]{2,1,0:T(8,128)(2,1)S(1)} %collective-permute-done.6.refs_5_), channel_id=1, source_target_pairs={{0,128},{128,0},{256,384},{384,256},{512,640},{640,512},{768,896},... | collective-permute-start | bytes 688136 | tf_op jit(solution)/shard_map/ppermute | solution.py:20
  75.1 9.1 %collective-permute-start.3 = (bf16[2,64,896]{2,1,0:T(8,128)(2,1)S(1)}, bf16[2,64,896]{2,1,0:T(8,128)(2,1)S(1)}, u32[]{:S(2)}, u32[]{:S(2)}) collective-permute-start(bf16[2,64,896]{2,1,0:T(8,128)(2,1)S(1)} %collective-permute-done.2.refs_2_), channel_id=1, source_target_pairs={{0,896},{896,0},{256,128},{128,256},{512,384},{384,512},{768,640},... | collective-permute-start | bytes 688136 | tf_op jit(solution)/shard_map/ppermute | solution.py:20

commit v5 on v4

--- a/solution.py
+++ b/solution.py
@@ -1,3 +1,5 @@
+import functools
+
 import jax
 import jax.numpy as jnp
 from jax import lax
@@ -69,14 +71,17 @@
     return jnp.floor(scaled + 0.5).astype(jnp.int32).astype(jnp.int16)
 
 
-def inside_block(tile, ab_rows):
+def used_rows(irrep_ref, fill_ref, block, tile, ab_rows):
+    quad = lax.axis_index("y") * ZA + lax.axis_index("za")
+    left_over = fill_ref[irrep_ref[lax.axis_index("c")]] - (quad * QUAD + block) * ab_rows
     column = lax.broadcasted_iota(jnp.int32, (1, LANES), 1)
-    return jnp.where(column < ab_rows, tile, jnp.zeros((), jnp.float32))
+    return jnp.where(column < jnp.minimum(left_over, ab_rows), tile, jnp.zeros((), jnp.float32))
 
 
 def early_kernel(irrep_ref, fill_ref, *refs):
     pairs, blocks_ref = refs[: 4 * C - 1], refs[4 * C - 1]
-    out_ref, open_ref, left, right, held = refs[4 * C :]
+    out_ref, open_ref, first, left, second, held = refs[4 * C :]
+    right = (first, second)
     _, rows, cols = pairs[0].shape
     parts, ab_rows = blocks_ref.shape[1:3]
     y = lax.axis_index("y")
@@ -91,34 +96,32 @@
                 left[part, owner] = jnp.where(used, values, jnp.zeros((), values.dtype))
     for at in range(QUAD):
         for part in range(parts):
-            right[part, at, pl.ds(0, ab_rows)] = blocks_ref[at, part]
+            right[part][at, pl.ds(0, ab_rows)] = blocks_ref[at, part]
     for half in range(QUAD // 2):
         product = sum(
             lax.dot_general(
                 left[part].reshape(Y * rows, cols),
-                right[part, pl.ds(2 * half, 2)].reshape(2 * LANES, cols),
+                right[part][pl.ds(2 * half, 2)].reshape(2 * LANES, cols),
                 (((1,), (1,)), ((), ())),
                 preferred_element_type=jnp.float32,
             )
             for part in range(parts)
         )
         for side in range(2):
-            tile = inside_block(product[:, side * LANES : (side + 1) * LANES], ab_rows)
+            tile = product[:, side * LANES : (side + 1) * LANES]
+            tile = used_rows(irrep_ref, fill_ref, 2 * half + side, tile, ab_rows)
             held[...] = tile.reshape(Y, rows, LANES)
             for late in range(2):
                 open_ref[2 * half + side, late] = held[owner_of(y, 0, Y - 2 + late)]
             out_ref[2 * half + side] = as_integers(tile, ab_rows).reshape(Y, rows, LANES)
 
 
-def late_kernel(irrep_ref, fill_ref, last_ref, blocks_ref, early_ref, open_ref, out_ref, right):
+def late_kernel(ab_rows, irrep_ref, fill_ref, last_ref, right, early_ref, open_ref, out_ref):
     _, rows, cols = last_ref.shape
-    ab_rows = blocks_ref.shape[2]
     y = lax.axis_index("y")
     values = last_ref[...].reshape(2 * rows, cols)
     used = used_columns(irrep_ref, fill_ref, 0, cols)
     values = jnp.where(used, values, jnp.zeros((), values.dtype))
-    for at in range(QUAD):
-        right[at, pl.ds(0, ab_rows)] = blocks_ref[at, 0]
     out_ref[...] = early_ref[...]
     for half in range(QUAD // 2):
         product = lax.dot_general(
@@ -128,7 +131,8 @@
             preferred_element_type=jnp.float32,
         )
         for side in range(2):
-            tile = inside_block(product[:, side * LANES : (side + 1) * LANES], ab_rows)
+            tile = product[:, side * LANES : (side + 1) * LANES]
+            tile = used_rows(irrep_ref, fill_ref, 2 * half + side, tile, ab_rows)
             for late in range(2):
                 whole = tile[late * rows : (late + 1) * rows] + open_ref[2 * half + side, late]
                 out_ref[2 * half + side, owner_of(y, 0, Y - 2 + late)] = as_integers(whole, ab_rows)
@@ -139,14 +143,18 @@
     parts, ab_rows = blocks.shape[1:3]
     smem, vmem = pl.BlockSpec(memory_space=pltpu.SMEM), pl.BlockSpec(memory_space=pltpu.VMEM)
     whole = jax.ShapeDtypeStruct((QUAD, Y, rows, LANES), jnp.int16)
-    early, still_open = pl.pallas_call(
+    early, still_open, first = pl.pallas_call(
         early_kernel,
-        out_shape=(whole, jax.ShapeDtypeStruct((QUAD, 2, rows, LANES), jnp.float32)),
+        out_shape=(
+            whole,
+            jax.ShapeDtypeStruct((QUAD, 2, rows, LANES), jnp.float32),
+            jax.ShapeDtypeStruct((QUAD, LANES, cols), jnp.bfloat16),
+        ),
         in_specs=[smem] * 2 + [vmem] * len(pairs),
-        out_specs=[vmem] * 2,
+        out_specs=[vmem] * 3,
         scratch_shapes=[
             pltpu.VMEM((parts, Y, rows, cols), jnp.bfloat16),
-            pltpu.VMEM((parts, QUAD, LANES, cols), jnp.bfloat16),
+            pltpu.VMEM((QUAD, LANES, cols), jnp.bfloat16),
             pltpu.VMEM((Y, rows, LANES), jnp.float32),
         ],
         compiler_params=pltpu.CompilerParams(vmem_limit_bytes=24 * 2**20),
@@ -154,24 +162,19 @@
         name="early_ladder",
     )(batch_irrep, pair_fill, *pairs[:3], *pairs[4:], blocks)
     return pl.pallas_call(
-        late_kernel,
+        functools.partial(late_kernel, ab_rows),
         out_shape=whole,
         in_specs=[smem] * 2 + [vmem] * 4,
         out_specs=vmem,
-        scratch_shapes=[pltpu.VMEM((QUAD, LANES, cols), jnp.bfloat16)],
         compiler_params=pltpu.CompilerParams(vmem_limit_bytes=24 * 2**20),
         cost_estimate=pl.CostEstimate(flops=2**28, bytes_accessed=2 * 2**20, transcendentals=0),
         name="late_ladder",
-    )(batch_irrep, pair_fill, pairs[3], blocks, early, still_open)
-
-
-def total_kernel(irrep_ref, fill_ref, parts_ref, out_ref):
+    )(batch_irrep, pair_fill, pairs[3], first, early, still_open)
+
+
+def total_kernel(parts_ref, out_ref):
     batches, ab_rows, _ = out_ref.shape
     rows = parts_ref.shape[1]
-    place = lax.axis_index("y")
-    for axis, size in (("za", ZA), ("h", H), ("par", PAR)):
-        place = place * size + lax.axis_index(axis)
-    ab = place * ab_rows + lax.broadcasted_iota(jnp.int32, (ab_rows, 1), 0)
     for n in range(batches):
         classes = []
         for par in range(PAR):
@@ -185,19 +188,18 @@
         pieces = [
             classes[par][at * eight : (at + 1) * eight] for at in range(ZA * H) for par in range(PAR)
         ]
-        turned = jnp.concatenate(pieces, axis=0).T[:ab_rows]
-        out_ref[n] = jnp.where(ab < fill_ref[irrep_ref[n]], turned, jnp.zeros((), jnp.float32))
-
-
-def total_ladder(batch_irrep, pair_fill, parts, batches, ab_rows):
+        out_ref[n] = jnp.concatenate(pieces, axis=0).T[:ab_rows]
+
+
+def total_ladder(parts, batches, ab_rows):
     return pl.pallas_call(
         total_kernel,
         out_shape=jax.ShapeDtypeStruct((batches, ab_rows, PAR * parts.shape[1]), jnp.float32),
-        in_specs=[pl.BlockSpec(memory_space=pltpu.SMEM)] * 2 + [pl.BlockSpec(memory_space=pltpu.VMEM)],
+        in_specs=[pl.BlockSpec(memory_space=pltpu.VMEM)],
         out_specs=pl.BlockSpec(memory_space=pltpu.VMEM),
         cost_estimate=pl.CostEstimate(flops=2**20, bytes_accessed=2**20, transcendentals=0),
         name="total_ladder",
-    )(batch_irrep, pair_fill, parts)
+    )(parts)
 
 
 def on_device(amplitudes, integrals, batch_irrep, pair_fill):
@@ -227,7 +229,7 @@
     partial = partial_ladder(batch_irrep, pair_fill, pairs, blocks)
     partial = partial.reshape(-1, *partial.shape[2:])
     parts = lax.all_to_all(partial, ("h", "par", "x", "c"), 0, 0, tiled=True)
-    return total_ladder(batch_irrep, pair_fill, parts, batches, ab_rows).swapaxes(1, 2)
+    return total_ladder(parts, batches, ab_rows).swapaxes(1, 2)
 
 
 def solution(mesh):

time: 112 us -> 112 us (level)
  no operation moved by 1% of the time
where the time goes in v5:
time: 112 us
  starting transfers between devices  47.7 us (43%)
  waiting for transfers between devices  28.8 us (26%)
  blocking collectives  24.1 us (22%)
  Pallas kernels  9.36 us (8%)
  local copies, waits for them, and re-layouts  1.57 us (1%)
    all_to_all x1, blocking collectives, on_device(): parts = lax.all_to_all(partial, ('h', 'par', 'x', 'c'), 0, 0, tiled=True)  24.1 us
    ppermute x8, starting transfers between devices, trade(): return lax.ppermute(values, 'y', pairs)  23.8 us
    all_to_all x1, starting transfers between devices, on_device(): own = lax.all_to_all(spread, ('za', 'h', 'c'), 0, 0, tiled=True)  20.3 us
    all_to_all x1, waiting for transfers between devices, on_device(): own = lax.all_to_all(spread, ('za', 'h', 'c'), 0, 0, tiled=True)  16 us
    ppermute x8, waiting for transfers between devices, trade(): return lax.ppermute(values, 'y', pairs)  10.9 us
    all_to_all x1, starting transfers between devices, on_device(): lax.all_to_all(picked, ('h', 'par', 'c'), 0, 0, tiled=True)  3.66 us
    pallas_call x1, Pallas kernels, pick(): pl.pallas_call(pick_kernel, out_shape=jax.ShapeDtypeStruct((H, PAR, C, ab...  3.53 us
    pallas_call x1, Pallas kernels, partial_ladder(): pl.pallas_call(early_kernel, out_shape=(whole, jax.ShapeDtypeStruct((QUAD...  2.53 us
  transfers between devices with their start and end apart: 10, of which 9 were waited for; matrix products, arithmetic and copies ran while one was open for 0% of the time, Pallas kernels for 5%

profile of v5, /device:TPU:1, one launch (start us, length us, event | category | flops | bytes accessed | tf_op | source)
XLA Modules:
  0.0 111.6 jit_solution(8532976528713437430)
XLA Ops:
  0.0 0.8 copy.6
  1.5 20.3 %all-to-all-start = ((bf16[16,8,896]{2,1,0:T(8,128)(2,1)}), bf16[16,8,896]{2,1,0:T(8,128)(2,1)S(1)}, u32[]{:S(2)}, u32[]{:S(2)}) async-start(bf16[16,8,896]{2,1,0:T(8,128)(2,1)} %bitcast.2), calls=%async_computation | async-start | bytes 458752 | tf_op jit(solution)/shard_map/all_to_all | solution.py:212
  21.8 3.5 %pick_blocks.1 = bf16[2,2,2,112,896]{4,3,2,1,0:T(8,128)(2,1)} custom-call(s32[2]{0:T(128)} %irrep_ref.5, bf16[8,112,1792]{2,1,0:T(8,128)(2,1)} %integrals_ref.1), custom_call_target="tpu_custom_call" | custom-call | bytes 2097152 | tf_op jit(solution)/shard_map/pick_blocks/pallas_call | solution.py:49
  25.4 16.0 %all-to-all-done = bf16[16,8,896]{2,1,0:T(8,128)(2,1)S(1)} async-done(((bf16[16,8,896]{2,1,0:T(8,128)(2,1)}), bf16[16,8,896]{2,1,0:T(8,128)(2,1)S(1)}, u32[]{:S(2)}, u32[]{:S(2)}) %all-to-all-start) | async-done | bytes 229408 | tf_op jit(solution)/shard_map/all_to_all | solution.py:212
  41.3 3.7 %all-to-all-start.1 = ((bf16[8,112,896]{2,1,0:T(8,128)(2,1)}), bf16[8,112,896]{2,1,0:T(8,128)(2,1)S(1)}, u32[]{:S(2)}, u32[]{:S(2)}) async-start(bf16[8,112,896]{2,1,0:T(8,128)(2,1)} %bitcast.15), calls=%async_computation.1 | async-start | bytes 3211264 | tf_op jit(solution)/shard_map/all_to_all | solution.py:216
  45.0 5.1 %collective-permute-start.4 = (bf16[1,64,896]{2,1,0:T(8,128)(2,1)S(1)}, bf16[1,64,896]{2,1,0:T(8,128)(2,1)S(1)}, u32[]{:S(2)}, u32[]{:S(2)}) collective-permute-start(bf16[1,64,896]{2,1,0:T(8,128)(2,1)S(1)} %bitcast.19), channel_id=1, source_target_pairs={{0,896},{896,0},{256,128},{128,256},{512,384},{384,512},{768,640},... | collective-permute-start | bytes 344072 | tf_op jit(solution)/shard_map/ppermute | solution.py:22
  50.1 1.9 %collective-permute-start = (bf16[1,64,896]{2,1,0:T(8,128)(2,1)S(1)}, bf16[1,64,896]{2,1,0:T(8,128)(2,1)S(1)}, u32[]{:S(2)}, u32[]{:S(2)}) collective-permute-start(bf16[1,64,896]{2,1,0:T(8,128)(2,1)S(1)} %bitcast.17), channel_id=1, source_target_pairs={{0,128},{128,0},{256,384},{384,256},{512,640},{640,512},{768,896},... | collective-permute-start | bytes 344072 | tf_op jit(solution)/shard_map/ppermute | solution.py:22
  52.1 0.8 collective-permute-done.4
  52.9 2.5 %collective-permute-start.5 = (bf16[2,64,896]{2,1,0:T(8,128)(2,1)S(1)}, bf16[2,64,896]{2,1,0:T(8,128)(2,1)S(1)}, u32[]{:S(2)}, u32[]{:S(2)}) collective-permute-start(bf16[2,64,896]{2,1,0:T(8,128)(2,1)S(1)} %pad_maximum_fusion.1.refs_3_), channel_id=1, source_target_pairs={{0,128},{128,0},{256,384},{384,256},{512,640},{640,512},{768,896},... | collective-permute-start | bytes 688136 | tf_op jit(solution)/shard_map/ppermute | solution.py:22
  55.5 1.5 %collective-permute-done = bf16[1,64,896]{2,1,0:T(8,128)(2,1)S(1)} collective-permute-done((bf16[1,64,896]{2,1,0:T(8,128)(2,1)S(1)}, bf16[1,64,896]{2,1,0:T(8,128)(2,1)S(1)}, u32[]{:S(2)}, u32[]{:S(2)}) %collective-permute-start) | collective-permute-done | bytes 114720 | tf_op jit(solution)/shard_map/ppermute | solution.py:22
  57.0 2.7 %collective-permute-start.1 = (bf16[2,64,896]{2,1,0:T(8,128)(2,1)S(1)}, bf16[2,64,896]{2,1,0:T(8,128)(2,1)S(1)}, u32[]{:S(2)}, u32[]{:S(2)}) collective-permute-start(bf16[2,64,896]{2,1,0:T(8,128)(2,1)S(1)} %pad_maximum_fusion.refs_0_), channel_id=1, source_target_pairs={{0,896},{896,0},{256,128},{128,256},{512,384},{384,512},{768,640},... | collective-permute-start | bytes 688136 | tf_op jit(solution)/shard_map/ppermute | solution.py:22
  59.8 2.4 %collective-permute-done.5.refs_4_ = bf16[2,64,896]{2,1,0:T(8,128)(2,1)S(1)} collective-permute-done((bf16[2,64,896]{2,1,0:T(8,128)(2,1)S(1)}, bf16[2,64,896]{2,1,0:T(8,128)(2,1)S(1)}, u32[]{:S(2)}, u32[]{:S(2)}) %collective-permute-start.5) | collective-permute-done | bytes 229408 | tf_op jit(solution)/shard_map/ppermute | solution.py:22
  62.2 4.6 %collective-permute-start.6 = (bf16[2,64,896]{2,1,0:T(8,128)(2,1)S(1)}, bf16[2,64,896]{2,1,0:T(8,128)(2,1)S(1)}, u32[]{:S(2)}, u32[]{:S(2)}) collective-permute-start(bf16[2,64,896]{2,1,0:T(8,128)(2,1)S(1)} %collective-permute-done.5.refs_4_), channel_id=1, source_target_pairs={{0,896},{896,0},{256,128},{128,256},{512,384},{384,512},{768,640},... | collective-permute-start | bytes 688136 | tf_op jit(solution)/shard_map/ppermute | solution.py:22
  67.2 1.9 %collective-permute-start.2 = (bf16[2,64,896]{2,1,0:T(8,128)(2,1)S(1)}, bf16[2,64,896]{2,1,0:T(8,128)(2,1)S(1)}, u32[]{:S(2)}, u32[]{:S(2)}) collective-permute-start(bf16[2,64,896]{2,1,0:T(8,128)(2,1)S(1)} %collective-permute-done.1.refs_1_), channel_id=1, source_target_pairs={{0,128},{128,0},{256,384},{384,256},{512,640},{640,512},{768,896},... | collective-permute-start | bytes 688136 | tf_op jit(solution)/shard_map/ppermute | solution.py:22
  69.1 2.7 %collective-permute-done.6.refs_5_ = bf16[2,64,896]{2,1,0:T(8,128)(2,1)S(1)} collective-permute-done((bf16[2,64,896]{2,1,0:T(8,128)(2,1)S(1)}, bf16[2,64,896]{2,1,0:T(8,128)(2,1)S(1)}, u32[]{:S(2)}, u32[]{:S(2)}) %collective-permute-start.6) | collective-permute-done | bytes 229408 | tf_op jit(solution)/shard_map/ppermute | solution.py:22
  71.7 2.2 %collective-permute-start.7 = (bf16[2,64,896]{2,1,0:T(8,128)(2,1)S(1)}, bf16[2,64,896]{2,1,0:T(8,128)(2,1)S(1)}, u32[]{:S(2)}, u32[]{:S(2)}) collective-permute-start(bf16[2,64,896]{2,1,0:T(8,128)(2,1)S(1)} %collective-permute-done.6.refs_5_), channel_id=1, source_target_pairs={{0,128},{128,0},{256,384},{384,256},{512,640},{640,512},{768,896},... | collective-permute-start | bytes 688136 | tf_op jit(solution)/shard_map/ppermute | solution.py:22
  74.0 1.2 %collective-permute-done.2.refs_2_ = bf16[2,64,896]{2,1,0:T(8,128)(2,1)S(1)} collective-permute-done((bf16[2,64,896]{2,1,0:T(8,128)(2,1)S(1)}, bf16[2,64,896]{2,1,0:T(8,128)(2,1)S(1)}, u32[]{:S(2)}, u32[]{:S(2)}) %collective-permute-start.2) | collective-permute-done | bytes 229408 | tf_op jit(solution)/shard_map/ppermute | solution.py:22
  75.1 2.8 %collective-permute-start.3 = (bf16[2,64,896]{2,1,0:T(8,128)(2,1)S(1)}, bf16[2,64,896]{2,1,0:T(8,128)(2,1)S(1)}, u32[]{:S(2)}, u32[]{:S(2)}) collective-permute-start(bf16[2,64,896]{2,1,0:T(8,128)(2,1)S(1)} %collective-permute-done.2.refs_2_), channel_id=1, source_target_pairs={{0,896},{896,0},{256,128},{128,256},{512,384},{384,512},{768,640},... | collective-permute-start | bytes 688136 | tf_op jit(solution)/shard_map/ppermute | solution.py:22
  77.9 1.9 %collective-permute-done.7.refs_6_ = bf16[2,64,896]{2,1,0:T(8,128)(2,1)S(1)} collective-permute-done((bf16[2,64,896]{2,1,0:T(8,128)(2,1)S(1)}, bf16[2,64,896]{2,1,0:T(8,128)(2,1)S(1)}, u32[]{:S(2)}, u32[]{:S(2)}) %collective-permute-start.7) | collective-permute-done | bytes 229408 | tf_op jit(solution)/shard_map/ppermute | solution.py:22
  79.8 1.9 %all-to-all-done.1 = bf16[8,112,896]{2,1,0:T(8,128)(2,1)S(1)} async-done(((bf16[8,112,896]{2,1,0:T(8,128)(2,1)}), bf16[8,112,896]{2,1,0:T(8,128)(2,1)S(1)}, u32[]{:S(2)}, u32[]{:S(2)}) %all-to-all-start.1) | async-done | bytes 1605664 | tf_op jit(solution)/shard_map/all_to_all | solution.py:216
  81.7 2.5 %early_ladder.1 = (s16[4,8,64,128]{3,2,1,0:T(8,128)(2,1)S(1)}, f32[4,2,64,128]{3,2,1,0:T(8,128)S(1)}, bf16[4,128,896]{2,1,0:T(8,128)(2,1)S(1)}) custom-call(s32[2]{0:T(128)S(1)} %copy-done, s32[8]{0:T(128)S(1)} %copy-done.1, bf16[2,64,896]{2,1,0:T(8,128)(2,1)S(1)} %pad_maximum_fusion.refs_0_, bf16[2,64,896]{2,1,0:T(8,128)(2,1)S(1)} %collective-permute-done.1.refs_1_, ...), custom_call_target="tpu_custom_call" | custom-call | flops 1073741824 | bytes 6291456 | tf_op jit(solution)/shard_map/early_ladder/pallas_call | solution.py:146
  84.3 1.2 %late_ladder.1 = s16[4,8,64,128]{3,2,1,0:T(8,128)(2,1)S(1)} custom-call(s32[2]{0:T(128)S(1)} %copy-done, s32[8]{0:T(128)S(1)} %copy-done.1, bf16[2,64,896]{2,1,0:T(8,128)(2,1)S(1)} %collective-permute-done.3.last_ref, bf16[4,128,896]{2,1,0:T(8,128)(2,1)S(1)} %get-tuple-element.8.right, s16[4,8,64,128]{3,2,1,0:T(8,128)(2,1)S(1)} %get-tuple-element.9.early_ref, ...), custom_call_target="tpu_custom_call" | custom-call | flops 268435456 | bytes 2097152 | tf_op jit(solution)/shard_map/late_ladder/pallas_call | solution.py:164
  85.5 24.1 %all_to_all.15.parts_ref = s16[32,64,128]{2,1,0:T(8,128)(2,1)} all-to-all(s16[32,64,128]{2,1,0:T(8,128)(2,1)S(1)} %bitcast.13), channel_id=1, replica_groups=mesh['y'=8,'za'=4,'h'=2,'par'=2,'x'=4,'c'=2] {'h','par','x','c'}, dimensions={0} | all-to-all | bytes 1048576 | tf_op jit(solution)/shard_map/all_to_all | solution.py:231
  109.5 2.1 %total_ladder.1 = f32[2,112,128]{2,1,0:T(8,128)} custom-call(s16[32,64,128]{2,1,0:T(8,128)(2,1)} %all_to_all.15.parts_ref), custom_call_target="tpu_custom_call" | custom-call | flops 1048576 | bytes 1048576 | tf_op jit(solution)/shard_map/total_ladder/pallas_call | solution.py:195
  (10 shorter events, 1.2 us)
Async XLA Ops:
  1.5 39.8 %all-to-all-start = ((bf16[16,8,896]{2,1,0:T(8,128)(2,1)}), bf16[16,8,896]{2,1,0:T(8,128)(2,1)S(1)}, u32[]{:S(2)}, u32[]{:S(2)}) async-start(bf16[16,8,896]{2,1,0:T(8,128)(2,1)} %bitcast.2), calls=%async_computation | async-start | bytes 458752 | tf_op jit(solution)/shard_map/all_to_all | solution.py:212
  41.3 40.4 %copy-start = (s32[2]{0:T(128)S(1)}, s32[2]{0:T(128)}, u32[]{:S(2)}) copy-start(s32[2]{0:T(128)} %irrep_ref.5) | copy-start | bytes 28
  41.3 40.4 %copy-start.1 = (s32[8]{0:T(128)S(1)}, s32[8]{0:T(128)}, u32[]{:S(2)}) copy-start(s32[8]{0:T(128)} %fill_ref.3) | copy-start | bytes 100
  41.3 40.4 %all-to-all-start.1 = ((bf16[8,112,896]{2,1,0:T(8,128)(2,1)}), bf16[8,112,896]{2,1,0:T(8,128)(2,1)S(1)}, u32[]{:S(2)}, u32[]{:S(2)}) async-start(bf16[8,112,896]{2,1,0:T(8,128)(2,1)} %bitcast.15), calls=%async_computation.1 | async-start | bytes 3211264 | tf_op jit(solution)/shard_map/all_to_all | solution.py:216
  45.0 7.9 %collective-permute-start.4 = (bf16[1,64,896]{2,1,0:T(8,128)(2,1)S(1)}, bf16[1,64,896]{2,1,0:T(8,128)(2,1)S(1)}, u32[]{:S(2)}, u32[]{:S(2)}) collective-permute-start(bf16[1,64,896]{2,1,0:T(8,128)(2,1)S(1)} %bitcast.19), channel_id=1, source_target_pairs={{0,896},{896,0},{256,128},{128,256},{512,384},{384,512},{768,640},... | collective-permute-start | bytes 344072 | tf_op jit(solution)/shard_map/ppermute | solution.py:22
  50.1 6.9 %collective-permute-start = (bf16[1,64,896]{2,1,0:T(8,128)(2,1)S(1)}, bf16[1,64,896]{2,1,0:T(8,128)(2,1)S(1)}, u32[]{:S(2)}, u32[]{:S(2)}) collective-permute-start(bf16[1,64,896]{2,1,0:T(8,128)(2,1)S(1)} %bitcast.17), channel_id=1, source_target_pairs={{0,128},{128,0},{256,384},{384,256},{512,640},{640,512},{768,896},... | collective-permute-start | bytes 344072 | tf_op jit(solution)/shard_map/ppermute | solution.py:22
  52.9 9.2 %collective-permute-start.5 = (bf16[2,64,896]{2,1,0:T(8,128)(2,1)S(1)}, bf16[2,64,896]{2,1,0:T(8,128)(2,1)S(1)}, u32[]{:S(2)}, u32[]{:S(2)}) collective-permute-start(bf16[2,64,896]{2,1,0:T(8,128)(2,1)S(1)} %pad_maximum_fusion.1.refs_3_), channel_id=1, source_target_pairs={{0,128},{128,0},{256,384},{384,256},{512,640},{640,512},{768,896},... | collective-permute-start | bytes 688136 | tf_op jit(solution)/shard_map/ppermute | solution.py:22
  57.0 10.1 %collective-permute-start.1 = (bf16[2,64,896]{2,1,0:T(8,128)(2,1)S(1)}, bf16[2,64,896]{2,1,0:T(8,128)(2,1)S(1)}, u32[]{:S(2)}, u32[]{:S(2)}) collective-permute-start(bf16[2,64,896]{2,1,0:T(8,128)(2,1)S(1)} %pad_maximum_fusion.refs_0_), channel_id=1, source_target_pairs={{0,896},{896,0},{256,128},{128,256},{512,384},{384,512},{768,640},... | collective-permute-start | bytes 688136 | tf_op jit(solution)/shard_map/ppermute | solution.py:22
  62.2 9.6 %collective-permute-start.6 = (bf16[2,64,896]{2,1,0:T(8,128)(2,1)S(1)}, bf16[2,64,896]{2,1,0:T(8,128)(2,1)S(1)}, u32[]{:S(2)}, u32[]{:S(2)}) collective-permute-start(bf16[2,64,896]{2,1,0:T(8,128)(2,1)S(1)} %collective-permute-done.5.refs_4_), channel_id=1, source_target_pairs={{0,896},{896,0},{256,128},{128,256},{512,384},{384,512},{768,640},... | collective-permute-start | bytes 688136 | tf_op jit(solution)/shard_map/ppermute | solution.py:22
  67.2 8.0 %collective-permute-start.2 = (bf16[2,64,896]{2,1,0:T(8,128)(2,1)S(1)}, bf16[2,64,896]{2,1,0:T(8,128)(2,1)S(1)}, u32[]{:S(2)}, u32[]{:S(2)}) collective-permute-start(bf16[2,64,896]{2,1,0:T(8,128)(2,1)S(1)} %collective-permute-done.1.refs_1_), channel_id=1, source_target_pairs={{0,128},{128,0},{256,384},{384,256},{512,640},{640,512},{768,896},... | collective-permute-start | bytes 688136 | tf_op jit(solution)/shard_map/ppermute | solution.py:22
  71.7 8.1 %collective-permute-start.7 = (bf16[2,64,896]{2,1,0:T(8,128)(2,1)S(1)}, bf16[2,64,896]{2,1,0:T(8,128)(2,1)S(1)}, u32[]{:S(2)}, u32[]{:S(2)}) collective-permute-start(bf16[2,64,896]{2,1,0:T(8,128)(2,1)S(1)} %collective-permute-done.6.refs_5_), channel_id=1, source_target_pairs={{0,128},{128,0},{256,384},{384,256},{512,640},{640,512},{768,896},... | collective-permute-start | bytes 688136 | tf_op jit(solution)/shard_map/ppermute | solution.py:22
  75.1 9.1 %collective-permute-start.3 = (bf16[2,64,896]{2,1,0:T(8,128)(2,1)S(1)}, bf16[2,64,896]{2,1,0:T(8,128)(2,1)S(1)}, u32[]{:S(2)}, u32[]{:S(2)}) collective-permute-start(bf16[2,64,896]{2,1,0:T(8,128)(2,1)S(1)} %collective-permute-done.2.refs_2_), channel_id=1, source_target_pairs={{0,896},{896,0},{256,128},{128,256},{512,384},{384,512},{768,640},... | collective-permute-start | bytes 688136 | tf_op jit(solution)/shard_map/ppermute | solution.py:22
